TPU v7x, 256 devices: a whole 4x4x8 slice. The times are simulated.
256 devices in a mesh: leaf: 64 (over z, x, y_lo), sub: 4 (over y_hi, core).
Axes of the slice: x: 4, y: 4 (y_hi: 2, y_lo: 2; y = y_hi * 2 + y_lo), z: 8, core: 2. Of those that a mesh axis runs over, the one named last changes fastest.
Arguments:
- right_sides: bfloat16 [64, 262144], P(None, ('leaf', 'sub')), may hold values from -6 to 6
- leaf_basis: bfloat16 [64, 262144], P(None, ('leaf', 'sub')), may hold values from -0.75 to 0.75
- near_blocks: bfloat16 [4096, 8, 4096], P(('leaf', 'sub')), may hold values from -0.25 to 0.25
- near_list: int32 [4096, 8], P(('leaf', 'sub')), may hold values from 0 to 4095, as said below
- local_transfer: bfloat16 [7936, 4096], P(('leaf', 'sub')), may hold values from -0.5 to 0.5
- local_couple: bfloat16 [7936, 8, 4096], P(('leaf', 'sub')), may hold values from -0.375 to 0.375
- local_partner: int32 [7936, 8], P(('leaf', 'sub')), may hold values from 0 to 7935, as said below
- local_count: int32 [7936], P(('leaf', 'sub')), may hold values from 1 to 8, as said below
- group_transfer: bfloat16 [192, 4096], P('leaf'), may hold values from -0.5 to 0.5
- group_couple: bfloat16 [192, 4, 4096], P('leaf'), may hold values from -1 to 1
- group_partner: int32 [192, 4], P('leaf'), may hold values from 0 to 191, as said below
- group_count: int32 [192], P('leaf'), may hold values from 1 to 4, as said below
- top_transfer: bfloat16 [62, 4096], replicated, may hold values from -0.5 to 0.5
- top_couple: bfloat16 [63, 3, 4096], replicated, may hold values from -1 to 1
- top_partner: int32 [63, 3], replicated, may hold values from 0 to 62, as said below
- top_count: int32 [63], replicated, may hold values from 0 to 3, as said below
Outputs:
- product: float32 [64, 262144], P(None, ('leaf', 'sub'))
Inputs may be any that keep to these rules, and one draw needn't show every extreme that they name: `near_list`: entry (t, k) names a leaf at most 8 places from leaf t in tree order. `local_partner`: entry (c, k) names a cluster of the same level as c, other than c, in c's own subtree or in the subtree just before or just after it. Only the first local_count slots of row c are used; in every subtree some cluster uses all 8. `group_partner`: entry (c, k) names a group cluster of the same level as c, other than c, in c's group or in the group just before or just after it. Only the first group_count slots of row c are used; some cluster uses all 4. `top_partner`: entry (c, k) names a top cluster of the same level as c, other than c; the root names itself. Only the first top_count slots of row c are used; a count is below the number of clusters on c's level, so the root has none; some cluster of the first top level uses all 3.
All inputs are finite; a program needn't handle non-finite values.
Results may differ from a plain program's by a relative error of at most 0.024.
Values may be sent and summed in bfloat16 or wider, within the bound.
A program may use at most 128 MiB of HBM per device.

v0:
```python
import jax
import jax.numpy as jnp
from jax import lax
from jax.sharding import PartitionSpec as P

LEAF = 64
RANK = 64
RHS = 64
NEARW = 8


def padded_2(array, sides, width):
    for axis, dim in sides:
        size, length = (lax.axis_size(axis), array.shape[dim])
        up = [(i, (i + 1) % size) for i in range(size - 1)]
        down = [(j, i) for i, j in up]
        last = lax.slice_in_dim(array, length - width, length, axis=dim)
        initial = lax.slice_in_dim(array, 0, width, axis=dim)
        before = lax.ppermute(last, axis, up)
        after = lax.ppermute(initial, axis, down)
        array = jnp.concatenate([before, array, after], axis=dim)
    return array


def blocks(packed, height, across):
    return packed.reshape(packed.shape[:-1] + (height, across))


def ladder(number):
    pieces = []
    offset = 0
    while number >= 1:
        pieces.append((offset, number))
        offset = offset + number
        number = number // 2
    return pieces


def pair_sum(values):
    return values.reshape((values.shape[0] // 2, 2) + values.shape[1:]).sum(axis=1)


def couple_terms(source, couple, partner, counts):
    gathered = source[partner]
    slot_ids = lax.broadcasted_iota(jnp.int32, partner.shape, 1)
    active = slot_ids < counts[:, None]
    gathered = jnp.where(active[:, :, None, None], gathered, jnp.zeros_like(gathered))
    return jnp.einsum(
        "nkab,nkbr->nar", blocks(couple, RANK, RANK), gathered, preferred_element_type=jnp.float32
    )


def body(
    right_sides,
    leaf_basis,
    near_blocks,
    near_list,
    local_transfer,
    local_couple,
    local_partner,
    local_count,
    group_transfer,
    group_couple,
    group_partner,
    group_count,
    top_transfer,
    top_couple,
    top_partner,
    top_count,
):
    leaves = right_sides.shape[1] // LEAF
    clusters = 2 * leaves - 1
    near_reach = NEARW
    groups = lax.axis_size("leaf")
    group_id = lax.axis_index("leaf")
    member = lax.axis_index("sub")
    device = group_id * lax.axis_size("sub") + member
    padded = padded_2(right_sides, ((("leaf", "sub"), 1),), near_reach * LEAF)
    padded = padded.reshape(RHS, leaves + 2 * near_reach, LEAF)
    picked = padded[:, near_list - (device * leaves - near_reach)]
    near_part = jnp.einsum(
        "rtkp,tkqp->rtq",
        picked,
        blocks(near_blocks, LEAF, LEAF),
        preferred_element_type=jnp.float32,
    )
    basis_rows = leaf_basis.reshape(RANK, leaves, LEAF)
    leaf_coef = jnp.einsum(
        "klp,rlp->lkr",
        basis_rows,
        right_sides.reshape(RHS, leaves, LEAF),
        preferred_element_type=jnp.float32,
    ).astype(jnp.bfloat16)
    transfer = blocks(local_transfer, RANK, RANK)
    level_spans = ladder(leaves)
    levels = [leaf_coef]
    for offset, amount in level_spans[:-1]:
        lifted = jnp.einsum(
            "nab,nar->nbr",
            transfer[offset : offset + amount],
            levels[-1],
            preferred_element_type=jnp.float32,
        )
        levels.append(pair_sum(lifted).astype(jnp.bfloat16))
    own_table = jnp.concatenate(levels, axis=0).reshape(clusters, RANK * RHS)
    root_term = jnp.einsum(
        "ab,ar->br", transfer[clusters - 1], levels[-1][0], preferred_element_type=jnp.float32
    )
    local_table = padded_2(own_table, ((("leaf", "sub"), 0),), clusters)
    local_far = couple_terms(
        local_table.reshape(3 * clusters, RANK, RHS),
        local_couple,
        local_partner - (device - 1) * clusters,
        local_count,
    )
    own_trans = blocks(group_transfer, RANK, RANK)
    every_root = lax.all_gather(root_term[None], ("leaf", "sub"), axis=0, tiled=True)
    every_trans = blocks(
        lax.all_gather(group_transfer, "leaf", axis=0, tiled=True), RANK, RANK
    ).reshape(groups, 3, RANK, RANK)
    first_level = pair_sum(every_root).astype(jnp.bfloat16).reshape(groups, 2, RANK, RHS)
    second_level = jnp.einsum(
        "ghab,ghar->gbr", every_trans[:, :2], first_level, preferred_element_type=jnp.float32
    ).astype(jnp.bfloat16)
    group_table = jnp.concatenate([first_level, second_level[:, None]], axis=1).reshape(
        3 * groups, RANK, RHS
    )
    upper_terms = jnp.einsum(
        "gab,gar->gbr", every_trans[:, 2], second_level, preferred_element_type=jnp.float32
    )
    group_far = couple_terms(group_table, group_couple, group_partner, group_count)
    top_trans = blocks(top_transfer, RANK, RANK)
    top_spans = ladder(groups // 2)
    current = pair_sum(upper_terms).astype(jnp.bfloat16)
    top_levels = [current]
    for offset, amount in top_spans[:-1]:
        lifted = jnp.einsum(
            "nab,nar->nbr",
            top_trans[offset : offset + amount],
            current,
            preferred_element_type=jnp.float32,
        )
        current = pair_sum(lifted).astype(jnp.bfloat16)
        top_levels.append(current)
    top_table = jnp.concatenate(top_levels, axis=0)
    top_far = couple_terms(top_table, top_couple, top_partner, top_count)
    root_offset = top_spans[-1][0]
    descend = top_far[root_offset : root_offset + 1]
    for offset, amount in reversed(top_spans[:-1]):
        parent = jnp.repeat(descend.astype(jnp.bfloat16), 2, axis=0)
        descend = top_far[offset : offset + amount] + jnp.einsum(
            "nab,nbr->nar",
            top_trans[offset : offset + amount],
            parent,
            preferred_element_type=jnp.float32,
        )
    upper_down = lax.dynamic_index_in_dim(descend, group_id // 2, 0, keepdims=False)
    second_down = group_far[2] + jnp.einsum(
        "ab,br->ar",
        own_trans[2],
        upper_down.astype(jnp.bfloat16),
        preferred_element_type=jnp.float32,
    )
    first_down = group_far[:2] + jnp.einsum(
        "hab,br->har",
        own_trans[:2],
        second_down.astype(jnp.bfloat16),
        preferred_element_type=jnp.float32,
    )
    member_down = lax.dynamic_index_in_dim(first_down, member // 2, 0, keepdims=False)
    descend = (
        local_far[clusters - 1]
        + jnp.einsum(
            "ab,br->ar",
            transfer[clusters - 1],
            member_down.astype(jnp.bfloat16),
            preferred_element_type=jnp.float32,
        )
    )[None]
    for offset, amount in reversed(level_spans[:-1]):
        parent = jnp.repeat(descend.astype(jnp.bfloat16), 2, axis=0)
        descend = local_far[offset : offset + amount] + jnp.einsum(
            "nab,nbr->nar",
            transfer[offset : offset + amount],
            parent,
            preferred_element_type=jnp.float32,
        )
    far_part = jnp.einsum(
        "lkr,klp->rlp", descend.astype(jnp.bfloat16), basis_rows, preferred_element_type=jnp.float32
    )
    return (far_part + near_part).reshape(RHS, leaves * LEAF)


def solution(mesh):
    placed = (
        P(None, ("leaf", "sub")),
        P(None, ("leaf", "sub")),
        P(("leaf", "sub"), None, None),
        P(("leaf", "sub"), None),
        P(("leaf", "sub"), None),
        P(("leaf", "sub"), None, None),
        P(("leaf", "sub"), None),
        P(("leaf", "sub")),
        P("leaf", None),
        P("leaf", None, None),
        P("leaf", None),
        P("leaf"),
        P(),
        P(),
        P(),
        P(),
    )
    return jax.shard_map(
        body, mesh=mesh, in_specs=placed, out_specs=P(None, ("leaf", "sub")), check_vma=False
    )
```

profile of v0, /device:TPU:1, one launch (start us, length us, event | category | flops | bytes accessed | tf_op | source)
XLA Modules:
  0.0 787.2 jit_solution(110413178400336271)
XLA Ops:
  8.2 0.9 slice.130
  9.2 1.1 reshape.213
  10.3 1.1 reshape.212
  15.6 2.0 concatenate.25
  17.6 6.2 collective-permute-start
  23.8 1.9 collective-permute-start.1
  26.4 1.9 collective-permute-start.3
  28.3 5.3 collective-permute-start.2
  34.2 3.3 reshape.237
  37.5 6.9 reshape.217
  48.5 5.5 reshape.226
  54.0 1.3 slice.149
  55.3 1.0 slice.151
  60.7 1.4 reshape.236
  62.1 1.2 copy.118
  63.4 2.1 gather_fusion.3
  65.5 3.1 convolution_bitcast_fusion.1
  68.6 1.5 concatenate.26
  70.1 1.4 concatenate.27
  71.8 3.0 gather_fusion
  74.8 6.3 copy.105
  81.1 5.6 fusion.18
  86.8 181.5 %all-gather.7.cloned.1.call-done = bf16[64,3,4096]{2,1,0:T(4,128)(2,1)} async-done(((bf16[1,3,4096]{2,1,0:T(4,128)(2,1)}), bf16[64,3,4096]{2,1,0:T(4,128)(2,1)}) %all-gather.7.cloned.1.call-update) | async-done | bytes 1572880 | tf_op jit(solution)/shard_map/all_gather | solution.py:119
  268.3 2.7 copy.108
  271.0 4.4 reshape_reshape.3
  275.4 455.6 %all-gather.5.cloned.1.call-done = f32[16384,64]{1,0:T(8,128)} async-done(((f32[64,64]{1,0:T(8,128)}), f32[16384,64]{1,0:T(8,128)}) %all-gather.5.cloned.1.call-update) | async-done | bytes 4194320 | tf_op jit(solution)/shard_map/all_gather | solution.py:117
  731.0 5.0 reduce_sum.92
  736.0 3.3 copy.130
  739.2 5.3 copy.111
  744.5 2.3 bitcast_convert_fusion
  746.8 1.0 copy-done.14
  747.8 1.7 bitcast_reduce_fusion
  751.3 2.7 gather_fusion.2
  754.0 4.1 fusion.12
  758.1 1.3 copy-done.7
  759.5 1.6 copy.112
  761.1 2.2 pad_maximum_fusion
  763.3 2.7 gather_fusion.1
  766.9 1.0 fusion.36
  767.9 1.1 fusion.32
  769.0 1.1 fusion.28
  770.8 1.4 convolution_bitcast_fusion
  772.5 1.0 convolution_bitcast_fusion.10
  773.5 0.9 fusion.43
  774.4 1.0 fusion.37
  775.4 1.1 fusion.33
  776.5 1.1 fusion.29
  777.8 1.4 fusion.23
  (191 shorter events, 20.0 us)
Async XLA Ops:
  6.5 5.9 slice-start.5
  6.5 6.5 slice-start.6
  6.5 261.8 %all-gather.7.cloned.1.call-start = ((), (), s32[]{:S(2)}) async-start(), calls=%async_computation.1 | async-start | bytes 2129920 | tf_op jit(solution)/shard_map/all_gather | solution.py:119
  7.3 723.7 %all-gather.5.cloned.1.call-start = ((), (), s32[]{:S(2)}) async-start(), calls=%async_computation | async-start | bytes 8421376 | tf_op jit(solution)/shard_map/all_gather | solution.py:117
  9.1 4.4 copy-start.25
  9.2 5.8 copy-start.22
  11.7 5.8 copy-start.2
  11.7 14.0 %copy-start.12 = (bf16[64,1024]{1,0:T(8,128)(2,1)S(1)}, bf16[64,1024]{1,0:T(8,128)(2,1)}, u32[]{:S(2)}) copy-start(bf16[64,1024]{1,0:T(8,128)(2,1)} %param.16) | copy-start | bytes 393220
  11.7 21.9 %copy-start.30 = (bf16[3,4096]{1,0:T(4,128)(2,1)S(1)}, bf16[3,4096]{1,0:T(4,128)(2,1)}, u32[]{:S(2)}) copy-start(bf16[3,4096]{1,0:T(4,128)(2,1)} %param.24) | copy-start | bytes 73732
  12.0 21.6 %copy-start.13 = (bf16[62,4096]{1,0:T(8,128)(2,1)S(1)}, bf16[62,4096]{1,0:T(8,128)(2,1)}, u32[]{:S(2)}) copy-start(bf16[62,4096]{1,0:T(8,128)(2,1)} %param.28) | copy-start | bytes 1523716
  12.3 21.4 %copy-start.36 = (s32[16,8]{0,1:T(8,128)S(1)}, s32[16,8]{0,1:T(8,128)}, u32[]{:S(2)}) copy-start(s32[16,8]{0,1:T(8,128)} %param.19) | copy-start | bytes 1540
  12.3 21.6 %copy-start.38 = (s32[63,3]{0,1:T(4,128)S(1)}, s32[63,3]{0,1:T(4,128)}, u32[]{:S(2)}) copy-start(s32[63,3]{0,1:T(4,128)} %param.30) | copy-start | bytes 2272
  12.7 21.4 %copy-start.9 = (bf16[8,64,64]{2,1,0:T(8,128)(2,1)}, bf16[8,64,64]{2,1,0:T(8,128)(2,1)S(1)}, u32[]{:S(2)}) copy-start(bf16[8,64,64]{2,1,0:T(8,128)(2,1)S(1)} %slice.133) | copy-start | bytes 196612
  13.0 24.4 %copy-start.15 = (bf16[4,64,64]{2,1,0:T(8,128)(2,1)}, bf16[4,64,64]{2,1,0:T(8,128)(2,1)S(1)}, u32[]{:S(2)}) copy-start(bf16[4,64,64]{2,1,0:T(8,128)(2,1)S(1)} %copy.98) | copy-start | bytes 98308
  13.2 24.3 %copy-start.17 = (bf16[4,64,64]{2,1,0:T(8,128)(2,1)}, bf16[4,64,64]{2,1,0:T(8,128)(2,1)S(1)}, u32[]{:S(2)}) copy-start(bf16[4,64,64]{2,1,0:T(8,128)(2,1)S(1)} %slice.135) | copy-start | bytes 98308
  13.5 24.0 %copy-start.20 = (bf16[2,64,64]{2,1,0:T(8,128)(2,1)}, bf16[2,64,64]{2,1,0:T(8,128)(2,1)S(1)}, u32[]{:S(2)}) copy-start(bf16[2,64,64]{2,1,0:T(8,128)(2,1)S(1)} %copy.100) | copy-start | bytes 49156
  17.6 51.0 %collective-permute-start = (bf16[31,4096]{1,0:T(8,128)(2,1)}, bf16[31,4096]{1,0:T(8,128)(2,1)}, u32[]{:S(2)}, u32[]{:S(2)}) collective-permute-start(bf16[31,4096]{1,0:T(8,128)(2,1)} %concatenate.25), channel_id=1, source_target_pairs={{0,1},{1,2},{2,3},{3,4},{4,5},{5,6},{6,7},{7,8},{8,9},{9,10},{10,1... | collective-permute-start | bytes 761864 | tf_op jit(solution)/shard_map/ppermute | solution.py:19
  23.8 46.3 %collective-permute-start.1 = (bf16[31,4096]{1,0:T(8,128)(2,1)}, bf16[31,4096]{1,0:T(8,128)(2,1)}, u32[]{:S(2)}, u32[]{:S(2)}) collective-permute-start(bf16[31,4096]{1,0:T(8,128)(2,1)} %concatenate.25), channel_id=1, source_target_pairs={{1,0},{2,1},{3,2},{4,3},{5,4},{6,5},{7,6},{8,7},{9,8},{10,9},{11,1... | collective-permute-start | bytes 761864 | tf_op jit(solution)/shard_map/ppermute | solution.py:20
  26.4 33.5 %collective-permute-start.3 = (bf16[64,512]{1,0:T(8,128)(2,1)}, bf16[64,512]{1,0:T(8,128)(2,1)}, u32[]{:S(2)}, u32[]{:S(2)}) collective-permute-start(bf16[64,512]{1,0:T(8,128)(2,1)} %get-tuple-element.6), channel_id=1, source_target_pairs={{1,0},{2,1},{3,2},{4,3},{5,4},{6,5},{7,6},{8,7},{9,8},{10,9},{11,1... | collective-permute-start | bytes 196616 | tf_op jit(solution)/shard_map/ppermute | solution.py:20
  28.3 31.5 %collective-permute-start.2 = (bf16[64,512]{1,0:T(8,128)(2,1)}, bf16[64,512]{1,0:T(8,128)(2,1)}, u32[]{:S(2)}, u32[]{:S(2)}) collective-permute-start(bf16[64,512]{1,0:T(8,128)(2,1)} %get-tuple-element.5), channel_id=1, source_target_pairs={{0,1},{1,2},{2,3},{3,4},{4,5},{5,6},{6,7},{7,8},{8,9},{9,10},{10,1... | collective-permute-start | bytes 196616 | tf_op jit(solution)/shard_map/ppermute | solution.py:19
  37.5 7.6 copy-start.37
  37.5 8.5 %copy-start.31 = (bf16[3,4096]{1,0:T(4,128)(2,1)S(1)}, bf16[3,4096]{1,0:T(4,128)(2,1)}, u32[]{:S(2)}) copy-start(bf16[3,4096]{1,0:T(4,128)(2,1)} %param.24) | copy-start | bytes 73732
  37.5 9.2 %copy-start.33 = (bf16[3,4,4096]{2,1,0:T(4,128)(2,1)S(1)}, bf16[3,4,4096]{2,1,0:T(4,128)(2,1)}, u32[]{:S(2)}) copy-start(bf16[3,4,4096]{2,1,0:T(4,128)(2,1)} %param.25) | copy-start | bytes 294916
  37.5 10.1 %copy-start.39 = (s32[3,4]{1,0:T(4,128)S(1)}, s32[3,4]{1,0:T(4,128)}, u32[]{:S(2)}) copy-start(s32[3,4]{1,0:T(4,128)} %param.26) | copy-start | bytes 148
  48.4 5.5 slice-start.1
  48.4 6.9 slice-start.2
  48.4 7.8 slice-start.3
  48.4 8.7 %slice-start.4 = ((bf16[62,4096]{1,0:T(8,128)(2,1)}), bf16[4,4096]{1,0:T(4,128)(2,1)S(1)}, s32[]{:S(2)}) async-start(bf16[62,4096]{1,0:T(8,128)(2,1)} %param.28), calls=%async_computation.6 | async-start | bytes 65536 | tf_op jit(solution)/shard_map/slice | solution.py:139
  48.5 9.4 %copy-start.42 = (s32[3]{0:T(128)S(1)}, s32[3]{0:T(128)}, u32[]{:S(2)}) copy-start(s32[3]{0:T(128)} %param.27) | copy-start | bytes 40
  48.5 10.0 %copy-start.40 = (s32[31]{0:T(128)S(1)}, s32[31]{0:T(128)}, u32[]{:S(2)}) copy-start(s32[31]{0:T(128)} %param.23) | copy-start | bytes 376
  48.5 10.1 %copy-start.41 = (s32[63]{0:T(128)S(1)}, s32[63]{0:T(128)}, u32[]{:S(2)}) copy-start(s32[63]{0:T(128)} %param.31) | copy-start | bytes 760
  68.6 3.1 copy-start.16
  68.6 3.1 copy-start.21
  68.6 3.1 copy-start.34
  751.3 2.7 copy-start.35
  763.3 6.9 copy-start.5
  763.3 7.0 copy-start.8
  766.1 4.7 copy-start.1
  770.3 1.9 copy-start.26
  770.3 1.9 copy-start.27
  770.3 1.9 copy-start.43
  770.3 2.2 copy-start.32
  770.6 2.9 copy-start.29
  770.6 3.8 copy-start.23
  770.6 4.8 copy-start.18
  770.8 5.8 copy-start.10
  770.8 7.0 copy-start.3
  770.8 7.0 copy-start.6
  (9 other events, 12.2 us)
Sparse Core Ops, SparseCore 0:
  9.1 259.0 all-gather.6
  270.2 460.7 all-gather.4
where the time goes:
time: 789 us; the launch traced here: 787 us
  waiting for transfers between devices  638 us (81%)
  local copies, waits for them, and re-layouts  78.6 us (10%)
  matrix products  30.8 us (4%)
  starting transfers between devices  15.4 us (2%)
  between operations  14.5 us (2%)
  other arithmetic  10.1 us (1%)
    all_gather x1, waiting for transfers between devices, body(): lax.all_gather(root_term[None], ('leaf', 'sub'), axis=0, tiled=True)  456 us
    all_gather x1, waiting for transfers between devices, body(): lax.all_gather(group_transfer, 'leaf', axis=0, tiled=True)  182 us
    reshape x4, local copies, waits for them, and re-layouts, blocks(): return packed.reshape(packed.shape[:-1] + (height, across))  16.5 us
  transfers between devices with their start and end apart: 6, of which 2 were waited for; matrix products, arithmetic and copies ran while one was open for 9% of the time, Pallas kernels for 0%

commit v1 on v0

v1 whole, which is shorter than its diff:
```python
import functools

import jax
import jax.numpy as jnp
from jax import lax
from jax.experimental import pallas as pl
from jax.experimental.pallas import tpu as pltpu
from jax.sharding import PartitionSpec as P

BF = jnp.bfloat16
F32 = jnp.float32
MESH = pl.DeviceIdType.MESH
TOP_OFF = (0, 32, 48, 56, 60, 62)
S_Q, S_X, S_Z, S_D, S_U, S_XH, S_TAB, S_GT, N_SEM = 0, 8, 12, 20, 28, 32, 34, 38, 40


def nt(a, b):
    return lax.dot_general(a, b, (((1,), (1,)), ((), ())), preferred_element_type=F32)


def nn(a, b):
    return jnp.dot(a, b, preferred_element_type=F32)


def half_swap(v):
    return pltpu.roll(v, 64, 1)


def iota(shape, dim):
    return lax.broadcasted_iota(jnp.int32, shape, dim)


def kernel(
    near_list_hbm, local_partner_hbm, local_count_hbm, group_partner_hbm, group_count_hbm, top_partner_hbm,
    top_count_hbm, x_hbm, basis_hbm, near_hbm, ltrans_hbm, lcouple_hbm, gtrans_hbm, gcouple_hbm, ttrans_hbm, tcouple_hbm,
    out,
    xs, bs, nb, lt, lc, gt_in, gc, tt, tc,
    ef, es, gf, ge, tf, et, sf, ts, bd, tab, bdt, xbd, pp, rl,
    qb, hr, p1, p2, p3, p4, ub, gu, gt, gs, zb, far, nearp, vht,
    near_list, local_partner, local_count, group_partner, group_count, top_partner, top_count,
    lsem, ssem, rsem,
):
    leaf = lax.axis_index("leaf")
    sub = lax.axis_index("sub")
    col, ylo = lax.div(leaf, 2), lax.rem(leaf, 2)
    z, x = lax.div(col, 4), lax.rem(col, 4)
    member = ylo * 4 + sub
    b = leaf * 4 + sub
    half = lax.div(sub, 2)

    relay = (ylo == 0) & (sub < 2)
    late = (ylo == 0) & (sub >= 2)

    def column_peer(m):
        return (col * 2 + lax.div(m, 4), lax.rem(m, 4))

    def ring_peer(step):
        n = lax.rem(b + step, 256)
        return (lax.div(n, 4), lax.rem(n, 4))

    col_peers = [column_peer(lax.rem(member + d, 8)) for d in range(8)]
    relays = [(col * 2, 0), (col * 2, 1)]
    x_peers = [((z * 4 + lax.rem(x + d, 4)) * 2 + ylo, sub) for d in range(4)]
    z_peers = [((lax.rem(z + d, 8) * 4 + x) * 2 + ylo, sub) for d in range(8)]
    sub_peers = [(leaf, lax.rem(sub + d, 4)) for d in range(4)]
    after, before = ring_peer(1), ring_peer(255)
    g_after = (lax.rem(leaf + 1, 64), sub)
    g_before = (lax.rem(leaf + 63, 64), sub)

    local = []

    def fetch(src, dst):
        cp = pltpu.make_async_copy(src, dst, lsem.at[len(local)])
        cp.start()
        local.append(cp)
        return cp

    w_x = [fetch(x_hbm.at[:, pl.ds(128 * m, 128)], xs.at[4 + m]) for m in range(8)]
    w_b = [fetch(basis_hbm, bs)]
    w_lt = [fetch(ltrans_hbm, lt)]
    w_gt = [fetch(gtrans_hbm, gt_in)]
    w_tt = [fetch(ttrans_hbm, tt)]
    w_tc = [fetch(tcouple_hbm, tc)]
    w_top = [fetch(top_partner_hbm, top_partner), fetch(top_count_hbm, top_count)]
    w_nb = [fetch(near_hbm, nb), fetch(near_list_hbm, near_list)]
    w_lc = [fetch(lcouple_hbm, lc), fetch(local_partner_hbm, local_partner), fetch(local_count_hbm, local_count)]
    w_gc = [fetch(gcouple_hbm, gc), fetch(group_partner_hbm, group_partner), fetch(group_count_hbm, group_count)]

    def ready(copies):
        for cp in copies:
            cp.wait()

    barrier = pltpu.get_barrier_semaphore()
    def greet(peers):
        for peer in peers:
            pl.semaphore_signal(barrier, inc=1, device_id=peer, device_id_type=MESH)

    greet(sub_peers[1:] + [after, before, g_after, g_before])

    @pl.when(relay)
    def _():
        greet(col_peers[1:] + x_peers[1:] + z_peers[1:])

    @pl.when(jnp.logical_not(relay))
    def _():
        greet(relays)

    def copy(src, dst, sent, got, peer):
        return pltpu.make_async_remote_copy(
            src_ref=src, dst_ref=dst, send_sem=ssem.at[sent], recv_sem=rsem.at[got],
            device_id=peer, device_id_type=MESH,
        )

    def send(src, dst, place, peer):
        cp = copy(src, dst, place, place, peer)
        cp.start()
        return cp

    lane = iota((1, 128), 1)
    left = lane < 64
    m_left = jnp.where(left, 1.0, 0.0).astype(BF)
    m_right = jnp.where(left, 0.0, 1.0).astype(BF)
    row, column = iota((128, 128), 0), iota((128, 128), 1)
    from_row = lax.div(row, 64) * 64 + 2 * lax.rem(row, 32) + lax.div(lax.rem(row, 64), 32)
    pp[...] = jnp.where(column == from_row, 1.0, 0.0).astype(BF)
    eye = jnp.where(iota((64, 64), 0) == iota((64, 64), 1), 1.0, 0.0).astype(BF)

    def unpack(load, n, dst, masked):
        if masked:
            cluster = iota((n, 128), 0)
            side = lax.rem(lax.div(cluster, 2), 2)
            if n == 31:
                side = jnp.where(cluster == 30, 0, side)
            lanes = iota((n, 128), 1)
            keep_l = (side == 0) & (lanes < 64)
            keep_r = (side == 1) & (lanes >= 64)
        for j in range(32):
            v = load(j).astype(F32)
            r = half_swap(v)
            if masked:
                zero = jnp.zeros_like(v)
                even = jnp.where(keep_l, v, jnp.where(keep_r, r, zero))
                odd = jnp.where(keep_l, r, jnp.where(keep_r, v, zero))
            else:
                even = jnp.where(left, v, r)
                odd = jnp.where(left, r, v)
            dst[pl.ds(2 * j, n, stride=64), :] = even
            dst[pl.ds(2 * j + 1, n, stride=64), :] = odd

    ready(w_x)
    ready(w_b)
    for m in range(8):
        two = bs[:, 128 * m : 128 * m + 128]
        both = jnp.concatenate([two * m_left, two * m_right], axis=0)
        bd[m] = both
        tab[16 + m] = nt(xs[4 + m], both).astype(BF)
    ready(w_lt)
    ready(w_gt)

    def upward():
        unpack(lambda j: lt[:, 128 * j : 128 * j + 128], 31, ef, True)
        es[...] = ef[...].astype(BF)
        unpack(lambda j: gt_in[:, 128 * j : 128 * j + 128], 3, gf, False)
        ge[...] = gf[...].astype(BF).reshape(3, 64, 128)
        e_root = es[30 * 64 : 31 * 64, :]
        pair_down = nn(ge[half][:, :64], ge[2]).astype(BF)
        h_root = nn(e_root[:, :64], pair_down).astype(BF)
        hr[...] = h_root
        for lo, hi, n in ((16, 24, 4), (24, 28, 2), (28, 30, 1)):
            for i in range(n):
                kids = jnp.concatenate([tab[lo + 2 * i], tab[lo + 2 * i + 1]], axis=1)
                first = 2 * (lo - 16) + 4 * i
                tab[hi + i] = nn(kids, es[first * 64 : first * 64 + 256, :]).astype(BF)
        c_root = nn(tab[30], es[28 * 64 : 30 * 64, :]).astype(BF)
        tab[31] = c_root
        q = nn(c_root[:, :64], h_root)
        qb[...] = q.reshape(2, 32, 128)
        ub[...] = nn(c_root[:, :64], e_root).astype(BF)

    def seen(l, first):
        mine = TOP_OFF[l] + lax.div(col, 2**l)
        total = jnp.zeros((64, 128), F32)
        for k in range(3):
            partner = jnp.where(k < top_count[mine], top_partner[k, mine], -1)
            target = jnp.where(left, first, first + 1)
            total = total + jnp.where(target == partner, gs[3 * l + k], 0.0)
        return total

    def prepare_top():
        unpack(lambda j: tt[:, 128 * j : 128 * j + 128], 62, tf, True)
        et[...] = tf[...].astype(BF)
        level_row, cluster_column = iota((8, 63), 0), iota((8, 63), 1)
        ancestor = level_row * 0 - 1
        for l in range(6):
            ancestor = jnp.where(level_row == l, TOP_OFF[l] + lax.div(col, 2**l), ancestor)
        pick = jnp.where(cluster_column == ancestor, 1.0, 0.0).astype(BF)
        for k in range(3):
            rows = nn(pick, tc[k])
            unpack(lambda j: rows[:, 128 * j : 128 * j + 128], 8, sf.at[pl.ds(512 * k, 512)], False)
        ts[...] = sf[...].astype(BF)
        path = None
        for l in range(6):
            for k in range(3):
                at = (8 * k + l) * 64
                gs[3 * l + k] = sf[at : at + 64, :] if l == 0 else nn(path[:, :64], ts[at : at + 64, :])
            if l < 5:
                place = pl.multiple_of((TOP_OFF[l] + lax.div(col, 2**l)) * 64, 64)
                step = et[pl.ds(place, 64), :]
                step = step + half_swap(step)
                path = step if l == 0 else nn(path[:, :64], step).astype(BF)
        level = [seen(5, 62).astype(BF)]
        for l in range(4, -1, -1):
            offset = TOP_OFF[l]
            lower_level = []
            for i, parents in enumerate(level):
                first = offset + 4 * i
                if l == 4:
                    w = et[first * 64 : (first + 2) * 64, :]
                    lower_level.append((nt(parents[:, :64], w[:, :64]) + seen(l, first)).astype(BF))
                else:
                    both = nt(parents, et[first * 64 : (first + 4) * 64, :])
                    lower_level.append((both[:, :128] + seen(l, first)).astype(BF))
                    lower_level.append((both[:, 128:] + seen(l, first + 2)).astype(BF))
            level = lower_level
        for i in range(16):
            zb[i] = level[i]

    ready(w_tt)
    ready(w_tc)
    ready(w_top)

    @pl.when(jnp.logical_not(late))
    def _():
        upward()

    @pl.when(relay)
    def _():
        prepare_top()

    pl.semaphore_wait(barrier, jnp.where(relay, 24, 9))
    leaves_own, upper_own = tab.at[pl.ds(16, 8)], tab.at[pl.ds(24, 8)]
    c_xh = [
        send(xs.at[pl.ds(8, 4)], xs.at[pl.ds(0, 4)], S_XH, after),
        send(xs.at[pl.ds(4, 4)], xs.at[pl.ds(12, 4)], S_XH + 1, before),
    ]
    c_leaves = [
        send(leaves_own, tab.at[pl.ds(0, 8)], S_TAB, after),
        send(leaves_own, tab.at[pl.ds(32, 8)], S_TAB + 1, before),
    ]

    @pl.when(late)
    def _():
        upward()

    c_q = [copy(qb.at[c], p1.at[member], S_Q + c, S_Q + member, relays[c]) for c in range(2)]
    for c in range(2):

        @pl.when(member != c)
        def _(c=c):
            c_q[c].start()

    c_u = [send(ub, gu.at[sub], S_U + d, sub_peers[d]) for d in range(1, 4)]
    c_upper = [
        send(upper_own, tab.at[pl.ds(8, 8)], S_TAB + 2, after),
        send(upper_own, tab.at[pl.ds(40, 8)], S_TAB + 3, before),
    ]
    gu[sub] = ub[...]

    def widen(src, dst, lo, n):
        def step(i, carry):
            for h in range(8):
                at = lo + 8 * i + h
                v = src[at]
                r = half_swap(v)
                dst[2 * at] = jnp.concatenate([v * m_left, r * m_right], axis=0)
                dst[2 * at + 1] = jnp.concatenate([r * m_left, v * m_right], axis=0)
            return carry

        lax.fori_loop(0, n, step, 0)

    def spread(load, n, ref):
        for j in range(32):
            ref[pl.ds(j, n, stride=32), :] = load(j).astype(F32)
        even, odd = [], []
        for k in range(0, n, 2):
            one, two = ref[32 * k : 32 * k + 32, :], ref[32 * k + 32 : 32 * k + 64, :]
            even.append(jnp.where(left, one, half_swap(two)))
            odd.append(jnp.where(left, half_swap(one), two))
        rows = [jnp.concatenate(even, axis=1), jnp.concatenate(odd, axis=1)]
        return jnp.concatenate(rows, axis=0).astype(BF)

    def coupled(table, ids, w):
        pairs = [table[ids[k], 0:64, :] + table[ids[k + 1], 64:128, :] for k in range(0, len(ids), 2)]
        return nt(jnp.concatenate(pairs, axis=1), w)

    def in_order(one, two):
        return nn(jnp.concatenate([one, two], axis=1).astype(BF), pp[...])

    ready(w_nb)
    widen(xs, xbd, 4, 1)
    for cp in c_xh:
        cp.wait_recv()
    for at in (0, 12):
        for h in range(4):
            v = xs[at + h]
            r = half_swap(v)
            xbd[2 * (at + h)] = jnp.concatenate([v * m_left, r * m_right], axis=0)
            xbd[2 * (at + h) + 1] = jnp.concatenate([r * m_left, v * m_right], axis=0)

    def near_step(i, carry):
        weights = []
        for h in range(8):
            t = 8 * i + h
            weights.append(spread(lambda j: nb[t, :, 128 * j : 128 * j + 128], 8, rl.at[h]))
        parts = []
        for h in range(8):
            ids = [jnp.clip(near_list[k, 8 * i + h] - (b * 16 - 8), 0, 31) for k in range(8)]
            parts.append(coupled(xbd, ids, weights[h]))
        for h in range(4):
            nearp[4 * i + h] = in_order(parts[2 * h], parts[2 * h + 1])
        return carry

    lax.fori_loop(0, 2, near_step, 0)

    c_z = [copy(p2.at[z], p2.at[z], S_Z + d, S_Z + d, z_peers[d]) for d in range(1, 8)]

    @pl.when(relay)
    def _():
        p1[member] = qb[member]
        for m in range(8):

            @pl.when(member != m)
            def _(m=m):
                copy(qb.at[0], p1.at[m], S_Q, S_Q + m, relays[0]).wait_recv()

        total = p1[0]
        for m in range(1, 8):
            total = total + p1[m]
        p2[z] = jnp.where(left, total[:16], total[16:]).astype(BF)
        for cp in c_z:
            cp.start()

    ready(w_lc)

    def far_step(i, carry):
        weights = []
        for h in range(8):
            c = jnp.minimum(8 * i + h, 30)
            weights.append(spread(lambda j: lc[c, :, 128 * j : 128 * j + 128], 8, rl.at[h]))
        parts = []
        for h in range(8):
            c = jnp.minimum(8 * i + h, 30)
            count = jnp.where(8 * i + h < 31, local_count[c], 0)
            ids = []
            for k in range(8):
                e = jnp.clip(local_partner[k, c] - (b - 1) * 31, 0, 92)
                e = e + jnp.where(e >= 31, 1, 0) + jnp.where(e >= 62, 1, 0)
                ids.append(jnp.where(k < count, e, 63))
            parts.append(coupled(bdt, ids, weights[h]))
        for h in range(4):
            far[4 * i + h] = in_order(parts[2 * h], parts[2 * h + 1])
        return carry

    widen(tab, bdt, 16, 2)
    for cp in c_leaves:
        cp.wait_recv()
    widen(tab, bdt, 0, 1)
    widen(tab, bdt, 32, 1)
    lax.fori_loop(0, 2, far_step, 0)

    c_x = [copy(p2, p3.at[x], S_X + d, S_X + d, x_peers[d]) for d in range(1, 4)]

    @pl.when(relay)
    def _():
        for cp in c_z:
            cp.wait_recv()
        for cp in c_x:
            cp.start()
        p3[x] = p2[...]

    for cp in c_u:
        cp.wait_recv()
    g0 = (gu[0].astype(F32) + gu[1].astype(F32)).astype(BF)
    g1 = (gu[2].astype(F32) + gu[3].astype(F32)).astype(BF)
    g2 = (nn(g0[:, :64], ge[0]) + nn(g1[:, :64], ge[1])).astype(BF)
    gt[3] = g0 + half_swap(g0)
    gt[4] = g1 + half_swap(g1)
    gt[5] = g2
    gt[9] = jnp.zeros((64, 128), BF)
    c_gt = [
        send(gt.at[pl.ds(3, 3)], gt.at[pl.ds(0, 3)], S_GT, g_after),
        send(gt.at[pl.ds(3, 3)], gt.at[pl.ds(6, 3)], S_GT + 1, g_before),
    ]

    for cp in c_upper:
        cp.wait_recv()
    widen(tab, bdt, 8, 1)
    widen(tab, bdt, 40, 1)
    lax.fori_loop(2, 4, far_step, 0)

    c_d = [copy(p4.at[sub], p4.at[sub], S_D + 1 + d, S_D + sub, col_peers[d]) for d in range(1, 8)]

    @pl.when(relay)
    def _():
        for cp in c_x:
            cp.wait_recv()
        have = []
        for i in range(16):
            one, two = p3[2 * (i % 2), i // 2], p3[2 * (i % 2) + 1, i // 2]
            up = one * m_left + half_swap(two) * m_right
            down = half_swap(one) * m_left + two * m_right
            have.append(jnp.concatenate([up, down], axis=0))
        weigh = jnp.concatenate([zb[i] for i in range(16)], axis=1)
        d = nt(jnp.concatenate(have, axis=1), weigh)
        p4[sub] = jnp.concatenate([d, d], axis=1).astype(BF)
        for cp in c_d:
            cp.start()

    ready(w_gc)
    for cp in c_gt:
        cp.wait_recv()
    found = []
    for c in range(3):
        w = spread(lambda j: gc[c, :, 128 * j : 128 * j + 128], 4, rl.at[c])
        entries = []
        for k in range(4):
            e = jnp.clip(group_partner[c, k] - (leaf - 1) * 3, 0, 8)
            entries.append(gt[jnp.where(k < group_count[c], e, 9)])
        pairs = [entries[k] * m_left + entries[k + 1] * m_right for k in (0, 2)]
        found.append(nt(jnp.concatenate(pairs, axis=1), w))
    f01 = in_order(found[0], found[1])
    f2 = in_order(found[2], found[2])
    f_half = jnp.where(half == 0, f01, half_swap(f01))[:, :64]
    d_half = f_half + nt(f2[:, :64].astype(BF), ge[half][:, :64])

    e_root = es[30 * 64 : 31 * 64, :]
    d_root = far[15][:, :64] + nt(d_half.astype(BF), e_root[:, :64])
    state = jnp.concatenate([d_root, nt(eye, hr[...][:, :64])], axis=0).astype(BF)
    nothing = jnp.zeros((64, 128), F32)

    def with_far(v, i):
        return (v + jnp.concatenate([far[i], nothing], axis=0)).astype(BF)

    states = [with_far(nt(state, es[28 * 64 : 30 * 64, :64]), 14)]
    for first, pair in ((24, 12), (16, 8), (0, 0)):
        lower_level = []
        for i, parents in enumerate(states):
            at = (first + 4 * i) * 64
            both = nt(parents, es[at : at + 256, :])
            lower_level.append(with_far(both[:, :128], pair + 2 * i))
            lower_level.append(with_far(both[:, 128:], pair + 2 * i + 1))
        states = lower_level
    for m in range(8):
        r = nn(states[m], bd[m])
        nearp[m] = nearp[m] + r[:64]
        vht[m] = r[64:].astype(BF)

    for c in range(2):

        @pl.when(member != c)
        def _(c=c):
            copy(p4.at[c], p4.at[c], S_D, S_D + c, relays[c]).wait_recv()

    d_col = p4[...].reshape(64, 128)[:, :64]
    for m in range(8):
        out[:, 128 * m : 128 * m + 128] = nearp[m] + nn(d_col, vht[m])

    for cp in c_u + c_xh + c_leaves + c_upper + c_gt:
        cp.wait_send()
    for c in range(2):

        @pl.when(member != c)
        def _(c=c):
            c_q[c].wait_send()

    @pl.when(relay)
    def _():
        for cp in c_z + c_x + c_d:
            cp.wait_send()


def body(
    right_sides, leaf_basis, near_blocks, near_list, local_transfer, local_couple, local_partner, local_count,
    group_transfer, group_couple, group_partner, group_count, top_transfer, top_couple, top_partner, top_count,
):
    hbm = pl.BlockSpec(memory_space=pltpu.HBM)
    vm = pltpu.VMEM
    return pl.pallas_call(
        kernel,
        out_shape=jax.ShapeDtypeStruct((64, 1024), F32),
        in_specs=[hbm] * 16,
        out_specs=pl.BlockSpec(memory_space=pltpu.VMEM),
        scratch_shapes=[
            vm((16, 64, 128), BF),
            vm((64, 1024), BF),
            vm((16, 8, 4096), BF),
            vm((31, 4096), BF),
            vm((31, 8, 4096), BF),
            vm((3, 4096), BF),
            vm((3, 4, 4096), BF),
            vm((62, 4096), BF),
            vm((3, 63, 4096), BF),
            vm((31 * 64, 128), F32),
            vm((31 * 64, 128), BF),
            vm((3 * 64, 128), F32),
            vm((3, 64, 128), BF),
            vm((62 * 64, 128), F32),
            vm((62 * 64, 128), BF),
            vm((24 * 64, 128), F32),
            vm((24 * 64, 128), BF),
            vm((8, 128, 128), BF),
            vm((48, 64, 128), BF),
            vm((96, 128, 128), BF),
            vm((32, 128, 128), BF),
            vm((128, 128), BF),
            vm((8, 256, 128), F32),
            vm((2, 32, 128), F32),
            vm((64, 128), BF),
            vm((8, 32, 128), F32),
            vm((8, 16, 128), BF),
            vm((4, 8, 16, 128), BF),
            vm((2, 32, 128), BF),
            vm((64, 128), BF),
            vm((4, 64, 128), BF),
            vm((10, 64, 128), BF),
            vm((18, 64, 128), F32),
            vm((16, 64, 128), BF),
            vm((16, 64, 128), F32),
            vm((8, 64, 128), F32),
            vm((8, 64, 128), BF),
            pltpu.SMEM((8, 16), jnp.int32),
            pltpu.SMEM((8, 31), jnp.int32),
            pltpu.SMEM((31,), jnp.int32),
            pltpu.SMEM((3, 4), jnp.int32),
            pltpu.SMEM((3,), jnp.int32),
            pltpu.SMEM((3, 63), jnp.int32),
            pltpu.SMEM((63,), jnp.int32),
            pltpu.SemaphoreType.DMA((24,)),
            pltpu.SemaphoreType.DMA((N_SEM,)),
            pltpu.SemaphoreType.DMA((N_SEM,)),
        ],
        compiler_params=pltpu.CompilerParams(
            collective_id=0, has_side_effects=True, vmem_limit_bytes=60 * 1024 * 1024
        ),
        name="h2",
    )(
        near_list.T, local_partner.T, local_count, group_partner, group_count, top_partner.T, top_count,
        right_sides, leaf_basis, near_blocks, local_transfer, local_couple, group_transfer, group_couple,
        top_transfer, jnp.transpose(top_couple, (1, 0, 2)),
    )


def solution(mesh):
    both = ("leaf", "sub")
    placed = (
        P(None, both), P(None, both), P(both, None, None), P(both, None), P(both, None), P(both, None, None),
        P(both, None), P(both), P("leaf", None), P("leaf", None, None), P("leaf", None), P("leaf"),
        P(), P(), P(), P(),
    )
    return jax.shard_map(body, mesh=mesh, in_specs=placed, out_specs=P(None, both), check_vma=False)
```

time: 789 us -> 36.1 us (0.05)
  waiting for transfers between devices: 638 us -> 0 us
  local copies, waits for them, and re-layouts: 78.6 us -> 1.67 us
  Pallas kernels: 0 us -> 34 us
  matrix products: 30.8 us -> 0 us
  starting transfers between devices: 15.4 us -> 0 us
  between operations: 14.5 us -> 0.01 us
  other arithmetic: 10.1 us -> 0 us
    all_gather x2 -> x0, waiting for transfers between devices: 637 us -> none  [the longest x1 456 us: body(): lax.all_gather(root_term[None], ('leaf', 'sub'), axis=0, tiled=True)]
    pallas_call x0 -> x1, Pallas kernels: none -> 34 us  [body(): pl.pallas_call(kernel, out_shape=jax.ShapeDtypeStruct((64, 1024), F32), i...]
    dot_general x28 -> x0, matrix products: 30.8 us -> none  [the longest x3 9.96 us: couple_terms(): jnp.einsum('nkab,nkbr->nar', blocks(couple, RANK, RANK), gathered, prefer...]
    reshape x9 -> x0, local copies, waits for them, and re-layouts: 22.3 us -> none  [the longest x4 16.5 us: blocks(): return packed.reshape(packed.shape[:-1] + (height, across))]
    gather x6 -> x0, local copies, waits for them, and re-layouts: 17.7 us -> none  [the longest x5 15.6 us: couple_terms(): gathered = source[partner]]
    ppermute x4 -> x0, starting transfers between devices: 15.4 us -> none  [the longest x2 11.5 us: padded_2(): before = lax.ppermute(last, axis, up)]
    slice x32 -> x0, local copies, waits for them, and re-layouts: 8.57 us -> none  [the longest x14 4.64 us: body(): top_trans[offset:offset + amount]]
  transfers between devices with their start and end apart: 6 -> 0, of which waited for: 2 -> 0; matrix products, arithmetic and copies ran while one was open for 9% -> 0% of each run, Pallas kernels for 0% -> 0%
where the time goes in v1:
time: 36.1 us; the launch traced here: 35.7 us
  Pallas kernels  34 us (94%)
  local copies, waits for them, and re-layouts  1.67 us (5%)
    pallas_call x1, Pallas kernels, body(): pl.pallas_call(kernel, out_shape=jax.ShapeDtypeStruct((64, 1024), F32), i...  34 us
    unnamed x1, local copies, waits for them, and re-layouts  1.67 us

profile of v1, /device:TPU:1, one launch (start us, length us, event | category | flops | bytes accessed | tf_op | source)
XLA Modules:
  0.0 35.7 jit_solution(6679083265172537753)
XLA Ops:
  0.0 34.0 %h2.1 = f32[64,1024]{1,0:T(8,128)} custom-call(s32[8,16]{1,0:T(8,128)} %bitcast.5, s32[8,31]{1,0:T(8,128)} %bitcast.6, s32[31]{0:T(128)} %local_count_hbm.1, s32[3,4]{1,0:T(4,128)} %group_partner_hbm.1, s32[3]{0:T(128)} %group_count_hbm.1, s32[3,63]{1,0:T(4,128)} %bitcast.7, s32[63]{0:T(128)} %top_count_hbm.1, bf16[64,1024]{1,0:T(8,128)(2,1)} %x_hbm.1, ...), custom_call_target="tpu_custom_call" | custom-call | tf_op jit(solution)/shard_map/h2/pallas_call | solution.py:488
  34.0 1.7 %copy.18 = f32[64,1024]{1,0:T(8,128)} copy(f32[64,1024]{1,0:T(8,128)} %h2.1) | data formatting | bytes 524288

commit v2 on v1

--- a/solution.py
+++ b/solution.py
@@ -11,7 +11,7 @@
 F32 = jnp.float32
 MESH = pl.DeviceIdType.MESH
 TOP_OFF = (0, 32, 48, 56, 60, 62)
-S_Q, S_X, S_Z, S_D, S_U, S_XH, S_TAB, S_GT, N_SEM = 0, 8, 12, 20, 28, 32, 34, 38, 40
+S_Q, S_C, S_D, S_U, S_XH, S_TAB, S_GT, N_SEM = 0, 8, 12, 20, 24, 26, 30, 32
 
 
 def nt(a, b):
@@ -36,9 +36,9 @@
     out,
     xs, bs, nb, lt, lc, gt_in, gc, tt, tc,
     ef, es, gf, ge, tf, et, sf, ts, bd, tab, bdt, xbd, pp, rl,
-    qb, hr, p1, p2, p3, p4, ub, gu, gt, gs, zb, far, nearp, vht,
+    qb, hr, p1, p3, p4, ub, gu, gt, gs, zb, far, nearp, vht,
     near_list, local_partner, local_count, group_partner, group_count, top_partner, top_count,
-    lsem, ssem, rsem,
+    lsem, ssem, rsem, csem,
 ):
     leaf = lax.axis_index("leaf")
     sub = lax.axis_index("sub")
@@ -48,8 +48,7 @@
     b = leaf * 4 + sub
     half = lax.div(sub, 2)
 
-    relay = (ylo == 0) & (sub < 2)
-    late = (ylo == 0) & (sub >= 2)
+    source = member == z
 
     def column_peer(m):
         return (col * 2 + lax.div(m, 4), lax.rem(m, 4))
@@ -59,9 +58,8 @@
         return (lax.div(n, 4), lax.rem(n, 4))
 
     col_peers = [column_peer(lax.rem(member + d, 8)) for d in range(8)]
-    relays = [(col * 2, 0), (col * 2, 1)]
-    x_peers = [((z * 4 + lax.rem(x + d, 4)) * 2 + ylo, sub) for d in range(4)]
-    z_peers = [((lax.rem(z + d, 8) * 4 + x) * 2 + ylo, sub) for d in range(8)]
+    plane_peers = [(lax.rem(col + d, 32) * 2 + ylo, sub) for d in range(32)]
+    plane_sources = [((member * 4 + i) * 2 + ylo, sub) for i in range(4)]
     sub_peers = [(leaf, lax.rem(sub + d, 4)) for d in range(4)]
     after, before = ring_peer(1), ring_peer(255)
     g_after = (lax.rem(leaf + 1, 64), sub)
@@ -95,15 +93,15 @@
         for peer in peers:
             pl.semaphore_signal(barrier, inc=1, device_id=peer, device_id_type=MESH)
 
-    greet(sub_peers[1:] + [after, before, g_after, g_before])
-
-    @pl.when(relay)
+    greet(col_peers[1:] + [after, before, g_after, g_before])
+
+    @pl.when(source)
     def _():
-        greet(col_peers[1:] + x_peers[1:] + z_peers[1:])
-
-    @pl.when(jnp.logical_not(relay))
+        greet(plane_peers[1:])
+
+    @pl.when(jnp.logical_not(source))
     def _():
-        greet(relays)
+        greet(plane_sources)
 
     def copy(src, dst, sent, got, peer):
         return pltpu.make_async_remote_copy(
@@ -174,7 +172,7 @@
         c_root = nn(tab[30], es[28 * 64 : 30 * 64, :]).astype(BF)
         tab[31] = c_root
         q = nn(c_root[:, :64], h_root)
-        qb[...] = q.reshape(2, 32, 128)
+        qb[...] = jnp.where(left, q[:32], q[32:]).astype(BF)
         ub[...] = nn(c_root[:, :64], e_root).astype(BF)
 
     def seen(l, first):
@@ -187,15 +185,23 @@
         return total
 
     def prepare_top():
-        unpack(lambda j: tt[:, 128 * j : 128 * j + 128], 62, tf, True)
+        wanted = [60 + lax.div(member, 4), 56 + lax.div(member, 2), 48 + member]
+        wanted += [32 + 2 * member + i for i in range(2)] + [4 * member + i for i in range(4)]
+        wanted += [TOP_OFF[l] + lax.div(col, 2**l) for l in range(5)]
+
+        def pick(rows, n, clusters):
+            at = iota((rows, n), 0)
+            cluster = at * 0 - 1
+            for i, c in enumerate(clusters):
+                cluster = jnp.where(at == i, c, cluster)
+            return jnp.where(iota((rows, n), 1) == cluster, 1.0, 0.0).astype(BF)
+
+        rows = nn(pick(16, 62, wanted), tt[...])
+        unpack(lambda j: rows[:, 128 * j : 128 * j + 128], 16, tf, False)
         et[...] = tf[...].astype(BF)
-        level_row, cluster_column = iota((8, 63), 0), iota((8, 63), 1)
-        ancestor = level_row * 0 - 1
-        for l in range(6):
-            ancestor = jnp.where(level_row == l, TOP_OFF[l] + lax.div(col, 2**l), ancestor)
-        pick = jnp.where(cluster_column == ancestor, 1.0, 0.0).astype(BF)
+        ancestors = pick(8, 63, [TOP_OFF[l] + lax.div(col, 2**l) for l in range(6)])
         for k in range(3):
-            rows = nn(pick, tc[k])
+            rows = nn(ancestors, tc[k])
             unpack(lambda j: rows[:, 128 * j : 128 * j + 128], 8, sf.at[pl.ds(512 * k, 512)], False)
         ts[...] = sf[...].astype(BF)
         path = None
@@ -204,67 +210,70 @@
                 at = (8 * k + l) * 64
                 gs[3 * l + k] = sf[at : at + 64, :] if l == 0 else nn(path[:, :64], ts[at : at + 64, :])
             if l < 5:
-                place = pl.multiple_of((TOP_OFF[l] + lax.div(col, 2**l)) * 64, 64)
-                step = et[pl.ds(place, 64), :]
-                step = step + half_swap(step)
+                step = et[(9 + l) * 64 : (10 + l) * 64, :]
                 path = step if l == 0 else nn(path[:, :64], step).astype(BF)
-        level = [seen(5, 62).astype(BF)]
-        for l in range(4, -1, -1):
-            offset = TOP_OFF[l]
-            lower_level = []
-            for i, parents in enumerate(level):
-                first = offset + 4 * i
-                if l == 4:
-                    w = et[first * 64 : (first + 2) * 64, :]
-                    lower_level.append((nt(parents[:, :64], w[:, :64]) + seen(l, first)).astype(BF))
-                else:
-                    both = nt(parents, et[first * 64 : (first + 4) * 64, :])
-                    lower_level.append((both[:, :128] + seen(l, first)).astype(BF))
-                    lower_level.append((both[:, 128:] + seen(l, first + 2)).astype(BF))
-            level = lower_level
-        for i in range(16):
-            zb[i] = level[i]
-
-    ready(w_tt)
-    ready(w_tc)
-    ready(w_top)
-
-    @pl.when(jnp.logical_not(late))
+        v = seen(5, 62)
+        for i, l in enumerate((4, 3, 2)):
+            v = nt(v[:, :64].astype(BF), et[64 * i : 64 * i + 64, :64]) + seen(l, wanted[i])[:, :64]
+        v = nt(v.astype(BF), et[3 * 64 : 5 * 64, :64]) + seen(1, wanted[3])
+        w = jnp.concatenate([et[5 * 64 : 7 * 64, :] * m_left, et[7 * 64 : 9 * 64, :] * m_right], axis=0)
+        v = nt(v.astype(BF), w)
+        v = v + jnp.concatenate([seen(0, wanted[5]), seen(0, wanted[7])], axis=1)
+        zb[...] = v.astype(BF)
+
+    upward()
+    pl.semaphore_wait(barrier, jnp.where(source, 42, 15))
+
+    c_q = copy(qb, p1.at[member], S_Q, S_Q + member, column_peer(z))
+
+    @pl.when(jnp.logical_not(source))
     def _():
-        upward()
-
-    @pl.when(relay)
-    def _():
-        prepare_top()
-
-    pl.semaphore_wait(barrier, jnp.where(relay, 24, 9))
-    leaves_own, upper_own = tab.at[pl.ds(16, 8)], tab.at[pl.ds(24, 8)]
+        c_q.start()
+
+    c_u = [send(ub, gu.at[sub], S_U + d, sub_peers[d]) for d in range(1, 4)]
+    gu[sub] = ub[...]
     c_xh = [
         send(xs.at[pl.ds(8, 4)], xs.at[pl.ds(0, 4)], S_XH, after),
         send(xs.at[pl.ds(4, 4)], xs.at[pl.ds(12, 4)], S_XH + 1, before),
     ]
+    leaves_own, upper_own = tab.at[pl.ds(16, 8)], tab.at[pl.ds(24, 8)]
     c_leaves = [
         send(leaves_own, tab.at[pl.ds(0, 8)], S_TAB, after),
         send(leaves_own, tab.at[pl.ds(32, 8)], S_TAB + 1, before),
     ]
-
-    @pl.when(late)
-    def _():
-        upward()
-
-    c_q = [copy(qb.at[c], p1.at[member], S_Q + c, S_Q + member, relays[c]) for c in range(2)]
-    for c in range(2):
-
-        @pl.when(member != c)
-        def _(c=c):
-            c_q[c].start()
-
-    c_u = [send(ub, gu.at[sub], S_U + d, sub_peers[d]) for d in range(1, 4)]
     c_upper = [
         send(upper_own, tab.at[pl.ds(8, 8)], S_TAB + 2, after),
         send(upper_own, tab.at[pl.ds(40, 8)], S_TAB + 3, before),
     ]
-    gu[sub] = ub[...]
+
+    ready(w_tt)
+    ready(w_tc)
+    ready(w_top)
+    prepare_top()
+
+    c_c = [
+        pltpu.make_async_remote_copy(
+            src_ref=p3.at[x], dst_ref=p3.at[x], send_sem=csem.at[d], recv_sem=rsem.at[S_C + x],
+            device_id=plane_peers[d], device_id_type=MESH,
+        )
+        for d in range(1, 32)
+    ]
+
+    @pl.when(source)
+    def _():
+        p1[member] = qb[...]
+        for m in range(8):
+
+            @pl.when(member != m)
+            def _(m=m):
+                copy(qb, p1.at[m], S_Q, S_Q + m, col_peers[1]).wait_recv()
+
+        total = p1[0].astype(F32)
+        for m in range(1, 8):
+            total = total + p1[m].astype(F32)
+        p3[x] = total.astype(BF)
+        for cp in c_c:
+            cp.start()
 
     def widen(src, dst, lo, n):
         def step(i, carry):
@@ -322,23 +331,22 @@
 
     lax.fori_loop(0, 2, near_step, 0)
 
-    c_z = [copy(p2.at[z], p2.at[z], S_Z + d, S_Z + d, z_peers[d]) for d in range(1, 8)]
-
-    @pl.when(relay)
-    def _():
-        p1[member] = qb[member]
-        for m in range(8):
-
-            @pl.when(member != m)
-            def _(m=m):
-                copy(qb.at[0], p1.at[m], S_Q, S_Q + m, relays[0]).wait_recv()
-
-        total = p1[0]
-        for m in range(1, 8):
-            total = total + p1[m]
-        p2[z] = jnp.where(left, total[:16], total[16:]).astype(BF)
-        for cp in c_z:
-            cp.start()
+    c_d = [copy(p4.at[member], p4.at[member], S_D + d, S_D + d, col_peers[d]) for d in range(1, 8)]
+    for i in range(4):
+
+        @pl.when(jnp.logical_not(source & (x == i)))
+        def _(i=i):
+            copy(p3.at[i], p3.at[i], S_C, S_C + i, col_peers[1]).wait_recv()
+
+    have = []
+    for i in (0, 2):
+        up = p3[i] * m_left + half_swap(p3[i + 1]) * m_right
+        down = half_swap(p3[i]) * m_left + p3[i + 1] * m_right
+        have.append(jnp.concatenate([up, down], axis=0))
+    d = nt(jnp.concatenate(have, axis=1), zb[...])
+    p4[member] = jnp.concatenate([d[:32], d[32:]], axis=1).astype(BF)
+    for cp in c_d:
+        cp.start()
 
     ready(w_lc)
 
@@ -368,16 +376,6 @@
     widen(tab, bdt, 32, 1)
     lax.fori_loop(0, 2, far_step, 0)
 
-    c_x = [copy(p2, p3.at[x], S_X + d, S_X + d, x_peers[d]) for d in range(1, 4)]
-
-    @pl.when(relay)
-    def _():
-        for cp in c_z:
-            cp.wait_recv()
-        for cp in c_x:
-            cp.start()
-        p3[x] = p2[...]
-
     for cp in c_u:
         cp.wait_recv()
     g0 = (gu[0].astype(F32) + gu[1].astype(F32)).astype(BF)
@@ -397,24 +395,6 @@
     widen(tab, bdt, 8, 1)
     widen(tab, bdt, 40, 1)
     lax.fori_loop(2, 4, far_step, 0)
-
-    c_d = [copy(p4.at[sub], p4.at[sub], S_D + 1 + d, S_D + sub, col_peers[d]) for d in range(1, 8)]
-
-    @pl.when(relay)
-    def _():
-        for cp in c_x:
-            cp.wait_recv()
-        have = []
-        for i in range(16):
-            one, two = p3[2 * (i % 2), i // 2], p3[2 * (i % 2) + 1, i // 2]
-            up = one * m_left + half_swap(two) * m_right
-            down = half_swap(one) * m_left + two * m_right
-            have.append(jnp.concatenate([up, down], axis=0))
-        weigh = jnp.concatenate([zb[i] for i in range(16)], axis=1)
-        d = nt(jnp.concatenate(have, axis=1), weigh)
-        p4[sub] = jnp.concatenate([d, d], axis=1).astype(BF)
-        for cp in c_d:
-            cp.start()
 
     ready(w_gc)
     for cp in c_gt:
@@ -455,28 +435,26 @@
         nearp[m] = nearp[m] + r[:64]
         vht[m] = r[64:].astype(BF)
 
-    for c in range(2):
-
-        @pl.when(member != c)
-        def _(c=c):
-            copy(p4.at[c], p4.at[c], S_D, S_D + c, relays[c]).wait_recv()
-
-    d_col = p4[...].reshape(64, 128)[:, :64]
+    for cp in c_d:
+        cp.wait_recv()
+    total = p4[0].astype(F32)
+    for m in range(1, 8):
+        total = total + p4[m].astype(F32)
+    d_col = jnp.concatenate([total[:, :64], total[:, 64:]], axis=0).astype(BF)
     for m in range(8):
         out[:, 128 * m : 128 * m + 128] = nearp[m] + nn(d_col, vht[m])
 
-    for cp in c_u + c_xh + c_leaves + c_upper + c_gt:
+    for cp in c_u + c_xh + c_leaves + c_upper + c_gt + c_d:
         cp.wait_send()
-    for c in range(2):
-
-        @pl.when(member != c)
-        def _(c=c):
-            c_q[c].wait_send()
-
-    @pl.when(relay)
+
+    @pl.when(source)
     def _():
-        for cp in c_z + c_x + c_d:
+        for cp in c_c:
             cp.wait_send()
+
+    @pl.when(jnp.logical_not(source))
+    def _():
+        c_q.wait_send()
 
 
 def body(
@@ -504,8 +482,8 @@
             vm((31 * 64, 128), BF),
             vm((3 * 64, 128), F32),
             vm((3, 64, 128), BF),
-            vm((62 * 64, 128), F32),
-            vm((62 * 64, 128), BF),
+            vm((16 * 64, 128), F32),
+            vm((16 * 64, 128), BF),
             vm((24 * 64, 128), F32),
             vm((24 * 64, 128), BF),
             vm((8, 128, 128), BF),
@@ -514,17 +492,16 @@
             vm((32, 128, 128), BF),
             vm((128, 128), BF),
             vm((8, 256, 128), F32),
-            vm((2, 32, 128), F32),
+            vm((32, 128), BF),
             vm((64, 128), BF),
-            vm((8, 32, 128), F32),
-            vm((8, 16, 128), BF),
-            vm((4, 8, 16, 128), BF),
-            vm((2, 32, 128), BF),
+            vm((8, 32, 128), BF),
+            vm((4, 32, 128), BF),
+            vm((8, 32, 128), BF),
             vm((64, 128), BF),
             vm((4, 64, 128), BF),
             vm((10, 64, 128), BF),
             vm((18, 64, 128), F32),
-            vm((16, 64, 128), BF),
+            vm((64, 256), BF),
             vm((16, 64, 128), F32),
             vm((8, 64, 128), F32),
             vm((8, 64, 128), BF),
@@ -538,6 +515,7 @@
             pltpu.SemaphoreType.DMA((24,)),
             pltpu.SemaphoreType.DMA((N_SEM,)),
             pltpu.SemaphoreType.DMA((N_SEM,)),
+            pltpu.SemaphoreType.DMA((32,)),
         ],
         compiler_params=pltpu.CompilerParams(
             collective_id=0, has_side_effects=True, vmem_limit_bytes=60 * 1024 * 1024

time: 36.1 us -> 34.6 us (0.958)
  Pallas kernels: 34 us -> 32.5 us
    pallas_call x1, Pallas kernels: 34 us -> 32.5 us  [body(): pl.pallas_call(kernel, out_shape=jax.ShapeDtypeStruct((64, 1024), F32), i...]
where the time goes in v2:
time: 34.6 us; the launch traced here: 34.2 us
  Pallas kernels  32.5 us (94%)
  local copies, waits for them, and re-layouts  1.67 us (5%)
    pallas_call x1, Pallas kernels, body(): pl.pallas_call(kernel, out_shape=jax.ShapeDtypeStruct((64, 1024), F32), i...  32.5 us
    unnamed x1, local copies, waits for them, and re-layouts  1.67 us

profile of v2, /device:TPU:1, one launch (start us, length us, event | category | flops | bytes accessed | tf_op | source)
XLA Modules:
  0.0 34.2 jit_solution(6012033052308430614)
XLA Ops:
  0.0 32.5 %h2.1 = f32[64,1024]{1,0:T(8,128)} custom-call(s32[8,16]{1,0:T(8,128)} %bitcast.5, s32[8,31]{1,0:T(8,128)} %bitcast.6, s32[31]{0:T(128)} %local_count_hbm.1, s32[3,4]{1,0:T(4,128)} %group_partner_hbm.1, s32[3]{0:T(128)} %group_count_hbm.1, s32[3,63]{1,0:T(4,128)} %bitcast.7, s32[63]{0:T(128)} %top_count_hbm.1, bf16[64,1024]{1,0:T(8,128)(2,1)} %x_hbm.1, ...), custom_call_target="tpu_custom_call" | custom-call | tf_op jit(solution)/shard_map/h2/pallas_call | solution.py:466
  32.5 1.7 %copy.18 = f32[64,1024]{1,0:T(8,128)} copy(f32[64,1024]{1,0:T(8,128)} %h2.1) | data formatting | bytes 524288

commit v3 on v2

--- a/solution.py
+++ b/solution.py
@@ -11,7 +11,8 @@
 F32 = jnp.float32
 MESH = pl.DeviceIdType.MESH
 TOP_OFF = (0, 32, 48, 56, 60, 62)
-S_Q, S_C, S_D, S_U, S_XH, S_TAB, S_GT, N_SEM = 0, 8, 12, 20, 24, 26, 30, 32
+S_Q, S_C, S_D, S_U, S_GT, S_B, S_F, N_SEM = 0, 8, 12, 20, 24, 26, 38, 41
+HALO, LEAVES, UPPER = (0, 2, 8, 4, 0, 12, 16), (1, 4, 16, 16, 0, 32, 48), (2, 4, 24, 24, 8, 40, 52)
 
 
 def nt(a, b):
@@ -49,6 +50,9 @@
     half = lax.div(sub, 2)
 
     source = member == z
+    odd = lax.rem(member, 2)
+    other = 4 - 4 * ylo
+    far_after, far_before = lax.rem(member, 4) == 1, lax.rem(member, 4) == 2
 
     def column_peer(m):
         return (col * 2 + lax.div(m, 4), lax.rem(m, 4))
@@ -221,8 +225,58 @@
         v = v + jnp.concatenate([seen(0, wanted[5]), seen(0, wanted[7])], axis=1)
         zb[...] = v.astype(BF)
 
+    def peer_or(far, place, near):
+        peer = column_peer(place)
+        return tuple(jnp.where(far, a, c) for a, c in zip(peer, near))
+
+    def exchange(ref, kind):
+        k, n, to_after, to_before, from_before, from_after, kept = kind
+        copies = []
+        for h in range(2):
+            cp = copy(
+                ref.at[pl.ds(to_after + h * n, n)],
+                ref.at[pl.ds(jnp.where(far_after, kept, from_before + h * n), n)],
+                S_B + 4 * k + h,
+                jnp.where(far_after, S_F + k, S_B + 4 * k + h),
+                peer_or(far_after, other + 2 * h, after),
+            )
+            cp.start()
+            copies.append(cp)
+            cp = copy(
+                ref.at[pl.ds(to_before + h * n, n)],
+                ref.at[pl.ds(jnp.where(far_before, kept, from_after + h * n), n)],
+                S_B + 4 * k + 2 + h,
+                jnp.where(far_before, S_F + k, S_B + 4 * k + 2 + h),
+                peer_or(far_before, other + 2 * h + 1, before),
+            )
+            cp.start()
+            copies.append(cp)
+        return copies
+
+    def forward(ref, kind):
+        k, n, _, _, from_before, from_after, kept = kind
+        mine = ref.at[pl.ds(kept, n)]
+        copy(mine, mine, S_F + k, S_F + k, col_peers[1]).wait_recv()
+        cp = copy(
+            mine,
+            ref.at[pl.ds(jnp.where(odd == 1, from_after, from_before) + half * n, n)],
+            S_F + k,
+            S_B + 4 * k + 2 * odd + half,
+            column_peer(other + 2 - odd),
+        )
+        cp.start()
+        return cp
+
+    def arrived(ref, kind):
+        k, n, _, _, from_before, from_after, _ = kind
+        for side, first in enumerate((from_before, from_after)):
+            for h in range(2):
+                part = ref.at[pl.ds(first + h * n, n)]
+                copy(part, part, S_F, S_B + 4 * k + 2 * side + h, col_peers[1]).wait_recv()
+
+    pl.semaphore_wait(barrier, jnp.where(source, 42, 15))
+    c_bulk = exchange(xs, HALO) + exchange(tab, LEAVES)
     upward()
-    pl.semaphore_wait(barrier, jnp.where(source, 42, 15))
 
     c_q = copy(qb, p1.at[member], S_Q, S_Q + member, column_peer(z))
 
@@ -232,19 +286,8 @@
 
     c_u = [send(ub, gu.at[sub], S_U + d, sub_peers[d]) for d in range(1, 4)]
     gu[sub] = ub[...]
-    c_xh = [
-        send(xs.at[pl.ds(8, 4)], xs.at[pl.ds(0, 4)], S_XH, after),
-        send(xs.at[pl.ds(4, 4)], xs.at[pl.ds(12, 4)], S_XH + 1, before),
-    ]
-    leaves_own, upper_own = tab.at[pl.ds(16, 8)], tab.at[pl.ds(24, 8)]
-    c_leaves = [
-        send(leaves_own, tab.at[pl.ds(0, 8)], S_TAB, after),
-        send(leaves_own, tab.at[pl.ds(32, 8)], S_TAB + 1, before),
-    ]
-    c_upper = [
-        send(upper_own, tab.at[pl.ds(8, 8)], S_TAB + 2, after),
-        send(upper_own, tab.at[pl.ds(40, 8)], S_TAB + 3, before),
-    ]
+    c_upper = exchange(tab, UPPER)
+    c_forward = [forward(xs, HALO), forward(tab, LEAVES)]
 
     ready(w_tt)
     ready(w_tc)
@@ -274,6 +317,8 @@
         p3[x] = total.astype(BF)
         for cp in c_c:
             cp.start()
+
+    c_forward.append(forward(tab, UPPER))
 
     def widen(src, dst, lo, n):
         def step(i, carry):
@@ -307,8 +352,7 @@
 
     ready(w_nb)
     widen(xs, xbd, 4, 1)
-    for cp in c_xh:
-        cp.wait_recv()
+    arrived(xs, HALO)
     for at in (0, 12):
         for h in range(4):
             v = xs[at + h]
@@ -370,8 +414,7 @@
         return carry
 
     widen(tab, bdt, 16, 2)
-    for cp in c_leaves:
-        cp.wait_recv()
+    arrived(tab, LEAVES)
     widen(tab, bdt, 0, 1)
     widen(tab, bdt, 32, 1)
     lax.fori_loop(0, 2, far_step, 0)
@@ -390,8 +433,7 @@
         send(gt.at[pl.ds(3, 3)], gt.at[pl.ds(6, 3)], S_GT + 1, g_before),
     ]
 
-    for cp in c_upper:
-        cp.wait_recv()
+    arrived(tab, UPPER)
     widen(tab, bdt, 8, 1)
     widen(tab, bdt, 40, 1)
     lax.fori_loop(2, 4, far_step, 0)
@@ -444,7 +486,7 @@
     for m in range(8):
         out[:, 128 * m : 128 * m + 128] = nearp[m] + nn(d_col, vht[m])
 
-    for cp in c_u + c_xh + c_leaves + c_upper + c_gt + c_d:
+    for cp in c_bulk + c_upper + c_forward + c_u + c_gt + c_d:
         cp.wait_send()
 
     @pl.when(source)
@@ -469,7 +511,7 @@
         in_specs=[hbm] * 16,
         out_specs=pl.BlockSpec(memory_space=pltpu.VMEM),
         scratch_shapes=[
-            vm((16, 64, 128), BF),
+            vm((18, 64, 128), BF),
             vm((64, 1024), BF),
             vm((16, 8, 4096), BF),
             vm((31, 4096), BF),
@@ -487,7 +529,7 @@
             vm((24 * 64, 128), F32),
             vm((24 * 64, 128), BF),
             vm((8, 128, 128), BF),
-            vm((48, 64, 128), BF),
+            vm((56, 64, 128), BF),
             vm((96, 128, 128), BF),
             vm((32, 128, 128), BF),
             vm((128, 128), BF),

time: 34.6 us -> 36.8 us (1.064)
  Pallas kernels: 32.5 us -> 35.1 us
    pallas_call x1, Pallas kernels: 32.5 us -> 35.1 us  [body(): pl.pallas_call(kernel, out_shape=jax.ShapeDtypeStruct((64, 1024), F32), i...]
where the time goes in v3:
time: 36.8 us; the launch traced here: 36.7 us
  Pallas kernels  35.1 us (95%)
  local copies, waits for them, and re-layouts  1.67 us (5%)
    pallas_call x1, Pallas kernels, body(): pl.pallas_call(kernel, out_shape=jax.ShapeDtypeStruct((64, 1024), F32), i...  35.1 us
    unnamed x1, local copies, waits for them, and re-layouts  1.67 us

profile of v3, /device:TPU:1, one launch (start us, length us, event | category | flops | bytes accessed | tf_op | source)
XLA Modules:
  0.0 36.7 jit_solution(10581608628212255139)
XLA Ops:
  0.0 35.1 %h2.1 = f32[64,1024]{1,0:T(8,128)} custom-call(s32[8,16]{1,0:T(8,128)} %bitcast.5, s32[8,31]{1,0:T(8,128)} %bitcast.6, s32[31]{0:T(128)} %local_count_hbm.1, s32[3,4]{1,0:T(4,128)} %group_partner_hbm.1, s32[3]{0:T(128)} %group_count_hbm.1, s32[3,63]{1,0:T(4,128)} %bitcast.7, s32[63]{0:T(128)} %top_count_hbm.1, bf16[64,1024]{1,0:T(8,128)(2,1)} %x_hbm.1, ...), custom_call_target="tpu_custom_call" | custom-call | tf_op jit(solution)/shard_map/h2/pallas_call | solution.py:508
  35.1 1.7 %copy.18 = f32[64,1024]{1,0:T(8,128)} copy(f32[64,1024]{1,0:T(8,128)} %h2.1) | data formatting | bytes 524288

commit v4 on v2

--- a/solution.py
+++ b/solution.py
@@ -35,7 +35,7 @@
     top_count_hbm, x_hbm, basis_hbm, near_hbm, ltrans_hbm, lcouple_hbm, gtrans_hbm, gcouple_hbm, ttrans_hbm, tcouple_hbm,
     out,
     xs, bs, nb, lt, lc, gt_in, gc, tt, tc,
-    ef, es, gf, ge, tf, et, sf, ts, bd, tab, bdt, xbd, pp, rl,
+    es, ge, et, ts, bd, tab, bdt, xbd, pp,
     qb, hr, p1, p3, p4, ub, gu, gt, gs, zb, far, nearp, vht,
     near_list, local_partner, local_count, group_partner, group_count, top_partner, top_count,
     lsem, ssem, rsem, csem,
@@ -123,27 +123,30 @@
     pp[...] = jnp.where(column == from_row, 1.0, 0.0).astype(BF)
     eye = jnp.where(iota((64, 64), 0) == iota((64, 64), 1), 1.0, 0.0).astype(BF)
 
-    def unpack(load, n, dst, masked):
-        if masked:
-            cluster = iota((n, 128), 0)
-            side = lax.rem(lax.div(cluster, 2), 2)
-            if n == 31:
-                side = jnp.where(cluster == 30, 0, side)
-            lanes = iota((n, 128), 1)
-            keep_l = (side == 0) & (lanes < 64)
-            keep_r = (side == 1) & (lanes >= 64)
-        for j in range(32):
-            v = load(j).astype(F32)
-            r = half_swap(v)
-            if masked:
-                zero = jnp.zeros_like(v)
-                even = jnp.where(keep_l, v, jnp.where(keep_r, r, zero))
-                odd = jnp.where(keep_l, r, jnp.where(keep_r, v, zero))
-            else:
-                even = jnp.where(left, v, r)
-                odd = jnp.where(left, r, v)
-            dst[pl.ds(2 * j, n, stride=64), :] = even
-            dst[pl.ds(2 * j + 1, n, stride=64), :] = odd
+    def unpack(load):
+        parts = []
+        for lo in (0, 16):
+            tiles = []
+            for j in range(lo, lo + 16):
+                v = load(j)
+                tiles += [v, half_swap(v)]
+            parts.append(jnp.swapaxes(jnp.stack(tiles), 0, 1))
+        return lambda c: jnp.concatenate([part[c] for part in parts], axis=0).astype(BF)
+
+    def filled(v):
+        v = v.astype(F32)
+        if v.shape[0] == 8:
+            return v
+        return jnp.concatenate([v, jnp.zeros((8 - v.shape[0], 128), F32)], axis=0)
+
+    def on_left(v):
+        return v * m_left
+
+    def on_right(v):
+        return half_swap(v * m_left)
+
+    def on_both(v):
+        return on_left(v) + on_right(v)
 
     ready(w_x)
     ready(w_b)
@@ -156,10 +159,16 @@
     ready(w_gt)
 
     def upward():
-        unpack(lambda j: lt[:, 128 * j : 128 * j + 128], 31, ef, True)
-        es[...] = ef[...].astype(BF)
-        unpack(lambda j: gt_in[:, 128 * j : 128 * j + 128], 3, gf, False)
-        ge[...] = gf[...].astype(BF).reshape(3, 64, 128)
+        for lo in range(0, 31, 8):
+            hi = min(lo + 8, 31)
+            matrix = unpack(lambda j: filled(lt[lo:hi, 128 * j : 128 * j + 128]))
+            for c in range(lo, hi):
+                right = c < 30 and (c // 2) % 2 == 1
+                v = matrix(c - lo)
+                es[64 * c : 64 * c + 64, :] = on_right(v) if right else on_left(v)
+        matrix = unpack(lambda j: filled(gt_in[:, 128 * j : 128 * j + 128]))
+        for c in range(3):
+            ge[c] = on_both(matrix(c))
         e_root = es[30 * 64 : 31 * 64, :]
         pair_down = nn(ge[half][:, :64], ge[2]).astype(BF)
         h_root = nn(e_root[:, :64], pair_down).astype(BF)
@@ -197,18 +206,22 @@
             return jnp.where(iota((rows, n), 1) == cluster, 1.0, 0.0).astype(BF)
 
         rows = nn(pick(16, 62, wanted), tt[...])
-        unpack(lambda j: rows[:, 128 * j : 128 * j + 128], 16, tf, False)
-        et[...] = tf[...].astype(BF)
+        for lo in (0, 8):
+            matrix = unpack(lambda j: rows[lo : lo + 8, 128 * j : 128 * j + 128])
+            for c in range(lo, min(lo + 8, 14)):
+                v = matrix(c - lo)
+                et[64 * c : 64 * c + 64, :] = on_right(v) if c in (7, 8) else on_left(v) if c < 9 else on_both(v)
         ancestors = pick(8, 63, [TOP_OFF[l] + lax.div(col, 2**l) for l in range(6)])
         for k in range(3):
             rows = nn(ancestors, tc[k])
-            unpack(lambda j: rows[:, 128 * j : 128 * j + 128], 8, sf.at[pl.ds(512 * k, 512)], False)
-        ts[...] = sf[...].astype(BF)
+            matrix = unpack(lambda j: rows[:, 128 * j : 128 * j + 128])
+            for l in range(6):
+                ts[3 * l + k] = on_both(matrix(l))
         path = None
         for l in range(6):
             for k in range(3):
-                at = (8 * k + l) * 64
-                gs[3 * l + k] = sf[at : at + 64, :] if l == 0 else nn(path[:, :64], ts[at : at + 64, :])
+                s = ts[3 * l + k]
+                gs[3 * l + k] = s.astype(F32) if l == 0 else nn(path[:, :64], s)
             if l < 5:
                 step = et[(9 + l) * 64 : (10 + l) * 64, :]
                 path = step if l == 0 else nn(path[:, :64], step).astype(BF)
@@ -216,8 +229,7 @@
         for i, l in enumerate((4, 3, 2)):
             v = nt(v[:, :64].astype(BF), et[64 * i : 64 * i + 64, :64]) + seen(l, wanted[i])[:, :64]
         v = nt(v.astype(BF), et[3 * 64 : 5 * 64, :64]) + seen(1, wanted[3])
-        w = jnp.concatenate([et[5 * 64 : 7 * 64, :] * m_left, et[7 * 64 : 9 * 64, :] * m_right], axis=0)
-        v = nt(v.astype(BF), w)
+        v = nt(v.astype(BF), et[5 * 64 : 9 * 64, :])
         v = v + jnp.concatenate([seen(0, wanted[5]), seen(0, wanted[7])], axis=1)
         zb[...] = v.astype(BF)
 
@@ -287,12 +299,11 @@
 
         lax.fori_loop(0, n, step, 0)
 
-    def spread(load, n, ref):
-        for j in range(32):
-            ref[pl.ds(j, n, stride=32), :] = load(j).astype(F32)
+    def spread(load, n):
+        tiles = jnp.swapaxes(jnp.stack([load(j).astype(F32) for j in range(32)]), 0, 1)
         even, odd = [], []
         for k in range(0, n, 2):
-            one, two = ref[32 * k : 32 * k + 32, :], ref[32 * k + 32 : 32 * k + 64, :]
+            one, two = tiles[k], tiles[k + 1]
             even.append(jnp.where(left, one, half_swap(two)))
             odd.append(jnp.where(left, half_swap(one), two))
         rows = [jnp.concatenate(even, axis=1), jnp.concatenate(odd, axis=1)]
@@ -320,7 +331,7 @@
         weights = []
         for h in range(8):
             t = 8 * i + h
-            weights.append(spread(lambda j: nb[t, :, 128 * j : 128 * j + 128], 8, rl.at[h]))
+            weights.append(spread(lambda j: nb[t, :, 128 * j : 128 * j + 128], 8))
         parts = []
         for h in range(8):
             ids = [jnp.clip(near_list[k, 8 * i + h] - (b * 16 - 8), 0, 31) for k in range(8)]
@@ -354,7 +365,7 @@
         weights = []
         for h in range(8):
             c = jnp.minimum(8 * i + h, 30)
-            weights.append(spread(lambda j: lc[c, :, 128 * j : 128 * j + 128], 8, rl.at[h]))
+            weights.append(spread(lambda j: lc[c, :, 128 * j : 128 * j + 128], 8))
         parts = []
         for h in range(8):
             c = jnp.minimum(8 * i + h, 30)
@@ -401,7 +412,7 @@
         cp.wait_recv()
     found = []
     for c in range(3):
-        w = spread(lambda j: gc[c, :, 128 * j : 128 * j + 128], 4, rl.at[c])
+        w = spread(lambda j: gc[c, :, 128 * j : 128 * j + 128], 4)
         entries = []
         for k in range(4):
             e = jnp.clip(group_partner[c, k] - (leaf - 1) * 3, 0, 8)
@@ -478,20 +489,15 @@
             vm((3, 4, 4096), BF),
             vm((62, 4096), BF),
             vm((3, 63, 4096), BF),
-            vm((31 * 64, 128), F32),
             vm((31 * 64, 128), BF),
-            vm((3 * 64, 128), F32),
             vm((3, 64, 128), BF),
-            vm((16 * 64, 128), F32),
             vm((16 * 64, 128), BF),
-            vm((24 * 64, 128), F32),
-            vm((24 * 64, 128), BF),
+            vm((18, 64, 128), BF),
             vm((8, 128, 128), BF),
             vm((48, 64, 128), BF),
             vm((96, 128, 128), BF),
             vm((32, 128, 128), BF),
             vm((128, 128), BF),
-            vm((8, 256, 128), F32),
             vm((32, 128), BF),
             vm((64, 128), BF),
             vm((8, 32, 128), BF),

time: 34.6 us -> 33.5 us (0.968)
  the two profiles are of different devices: /device:TPU:1 before, /device:TPU:110 now
where the time goes in v4:
time: 33.5 us; the launch traced here: 33.4 us
  Pallas kernels  31.8 us (95%)
  local copies, waits for them, and re-layouts  1.67 us (5%)
    pallas_call x1, Pallas kernels, body(): pl.pallas_call(kernel, out_shape=jax.ShapeDtypeStruct((64, 1024), F32), i...  31.8 us
    unnamed x1, local copies, waits for them, and re-layouts  1.67 us

profile of v4, /device:TPU:110, one launch (start us, length us, event | category | flops | bytes accessed | tf_op | source)
XLA Modules:
  0.0 33.4 jit_solution(14279131685551266881)
XLA Ops:
  0.0 31.8 %h2.1 = f32[64,1024]{1,0:T(8,128)} custom-call(s32[8,16]{1,0:T(8,128)} %bitcast.5, s32[8,31]{1,0:T(8,128)} %bitcast.6, s32[31]{0:T(128)} %local_count_hbm.1, s32[3,4]{1,0:T(4,128)} %group_partner_hbm.1, s32[3]{0:T(128)} %group_count_hbm.1, s32[3,63]{1,0:T(4,128)} %bitcast.7, s32[63]{0:T(128)} %top_count_hbm.1, bf16[64,1024]{1,0:T(8,128)(2,1)} %x_hbm.1, ...), custom_call_target="tpu_custom_call" | custom-call | tf_op jit(solution)/shard_map/h2/pallas_call | solution.py:477
  31.8 1.7 %copy.18 = f32[64,1024]{1,0:T(8,128)} copy(f32[64,1024]{1,0:T(8,128)} %h2.1) | data formatting | bytes 524288

commit v5 on v4

--- a/solution.py
+++ b/solution.py
@@ -233,30 +233,31 @@
         v = v + jnp.concatenate([seen(0, wanted[5]), seen(0, wanted[7])], axis=1)
         zb[...] = v.astype(BF)
 
-    upward()
     pl.semaphore_wait(barrier, jnp.where(source, 42, 15))
-
-    c_q = copy(qb, p1.at[member], S_Q, S_Q + member, column_peer(z))
-
-    @pl.when(jnp.logical_not(source))
-    def _():
-        c_q.start()
-
-    c_u = [send(ub, gu.at[sub], S_U + d, sub_peers[d]) for d in range(1, 4)]
-    gu[sub] = ub[...]
     c_xh = [
         send(xs.at[pl.ds(8, 4)], xs.at[pl.ds(0, 4)], S_XH, after),
         send(xs.at[pl.ds(4, 4)], xs.at[pl.ds(12, 4)], S_XH + 1, before),
     ]
+    upward()
+
+    c_q = copy(qb, p1.at[member], S_Q, S_Q + member, column_peer(z))
     leaves_own, upper_own = tab.at[pl.ds(16, 8)], tab.at[pl.ds(24, 8)]
     c_leaves = [
-        send(leaves_own, tab.at[pl.ds(0, 8)], S_TAB, after),
-        send(leaves_own, tab.at[pl.ds(32, 8)], S_TAB + 1, before),
+        copy(leaves_own, tab.at[pl.ds(0, 8)], S_TAB, S_TAB, after),
+        copy(leaves_own, tab.at[pl.ds(32, 8)], S_TAB + 1, S_TAB + 1, before),
     ]
-    c_upper = [
-        send(upper_own, tab.at[pl.ds(8, 8)], S_TAB + 2, after),
-        send(upper_own, tab.at[pl.ds(40, 8)], S_TAB + 3, before),
-    ]
+
+    @pl.when(jnp.logical_not(source))
+    def _():
+        c_q.start()
+
+    c_u = [send(ub, gu.at[sub], S_U + d, sub_peers[d]) for d in range(1, 4)]
+    gu[sub] = ub[...]
+
+    @pl.when(jnp.logical_not(source))
+    def _():
+        for cp in c_leaves:
+            cp.start()
 
     ready(w_tt)
     ready(w_tc)
@@ -284,7 +285,7 @@
         for m in range(1, 8):
             total = total + p1[m].astype(F32)
         p3[x] = total.astype(BF)
-        for cp in c_c:
+        for cp in c_c + c_leaves:
             cp.start()
 
     def widen(src, dst, lo, n):
@@ -358,6 +359,25 @@
     p4[member] = jnp.concatenate([d[:32], d[32:]], axis=1).astype(BF)
     for cp in c_d:
         cp.start()
+
+    for cp in c_u:
+        cp.wait_recv()
+    g0 = (gu[0].astype(F32) + gu[1].astype(F32)).astype(BF)
+    g1 = (gu[2].astype(F32) + gu[3].astype(F32)).astype(BF)
+    g2 = (nn(g0[:, :64], ge[0]) + nn(g1[:, :64], ge[1])).astype(BF)
+    gt[3] = g0 + half_swap(g0)
+    gt[4] = g1 + half_swap(g1)
+    gt[5] = g2
+    gt[9] = jnp.zeros((64, 128), BF)
+    c_gt = [
+        send(gt.at[pl.ds(3, 3)], gt.at[pl.ds(0, 3)], S_GT, g_after),
+        send(gt.at[pl.ds(3, 3)], gt.at[pl.ds(6, 3)], S_GT + 1, g_before),
+    ]
+
+    c_upper = [
+        send(upper_own, tab.at[pl.ds(8, 8)], S_TAB + 2, after),
+        send(upper_own, tab.at[pl.ds(40, 8)], S_TAB + 3, before),
+    ]
 
     ready(w_lc)
 
@@ -386,20 +406,6 @@
     widen(tab, bdt, 0, 1)
     widen(tab, bdt, 32, 1)
     lax.fori_loop(0, 2, far_step, 0)
-
-    for cp in c_u:
-        cp.wait_recv()
-    g0 = (gu[0].astype(F32) + gu[1].astype(F32)).astype(BF)
-    g1 = (gu[2].astype(F32) + gu[3].astype(F32)).astype(BF)
-    g2 = (nn(g0[:, :64], ge[0]) + nn(g1[:, :64], ge[1])).astype(BF)
-    gt[3] = g0 + half_swap(g0)
-    gt[4] = g1 + half_swap(g1)
-    gt[5] = g2
-    gt[9] = jnp.zeros((64, 128), BF)
-    c_gt = [
-        send(gt.at[pl.ds(3, 3)], gt.at[pl.ds(0, 3)], S_GT, g_after),
-        send(gt.at[pl.ds(3, 3)], gt.at[pl.ds(6, 3)], S_GT + 1, g_before),
-    ]
 
     for cp in c_upper:
         cp.wait_recv()

time: 33.5 us -> 35.2 us (1.051)
  the two profiles are of different devices: /device:TPU:110 before, /device:TPU:1 now
where the time goes in v5:
time: 35.2 us; the launch traced here: 35.1 us
  Pallas kernels  33.4 us (95%)
  local copies, waits for them, and re-layouts  1.67 us (5%)
    pallas_call x1, Pallas kernels, body(): pl.pallas_call(kernel, out_shape=jax.ShapeDtypeStruct((64, 1024), F32), i...  33.4 us
    unnamed x1, local copies, waits for them, and re-layouts  1.67 us

profile of v5, /device:TPU:1, one launch (start us, length us, event | category | flops | bytes accessed | tf_op | source)
XLA Modules:
  0.0 35.1 jit_solution(3708732824723357188)
XLA Ops:
  0.0 33.4 %h2.1 = f32[64,1024]{1,0:T(8,128)} custom-call(s32[8,16]{1,0:T(8,128)} %bitcast.5, s32[8,31]{1,0:T(8,128)} %bitcast.6, s32[31]{0:T(128)} %local_count_hbm.1, s32[3,4]{1,0:T(4,128)} %group_partner_hbm.1, s32[3]{0:T(128)} %group_count_hbm.1, s32[3,63]{1,0:T(4,128)} %bitcast.7, s32[63]{0:T(128)} %top_count_hbm.1, bf16[64,1024]{1,0:T(8,128)(2,1)} %x_hbm.1, ...), custom_call_target="tpu_custom_call" | custom-call | tf_op jit(solution)/shard_map/h2/pallas_call | solution.py:483
  33.4 1.7 %copy.18 = f32[64,1024]{1,0:T(8,128)} copy(f32[64,1024]{1,0:T(8,128)} %h2.1) | data formatting | bytes 524288

commit v6 on v5

--- a/solution.py
+++ b/solution.py
@@ -238,13 +238,17 @@
         send(xs.at[pl.ds(8, 4)], xs.at[pl.ds(0, 4)], S_XH, after),
         send(xs.at[pl.ds(4, 4)], xs.at[pl.ds(12, 4)], S_XH + 1, before),
     ]
-    upward()
-
-    c_q = copy(qb, p1.at[member], S_Q, S_Q + member, column_peer(z))
     leaves_own, upper_own = tab.at[pl.ds(16, 8)], tab.at[pl.ds(24, 8)]
     c_leaves = [
-        copy(leaves_own, tab.at[pl.ds(0, 8)], S_TAB, S_TAB, after),
-        copy(leaves_own, tab.at[pl.ds(32, 8)], S_TAB + 1, S_TAB + 1, before),
+        send(leaves_own, tab.at[pl.ds(0, 8)], S_TAB, after),
+        send(leaves_own, tab.at[pl.ds(32, 8)], S_TAB + 1, before),
+    ]
+    upward()
+
+    c_q = copy(qb, p1.at[member], S_Q, S_Q + member, column_peer(z))
+    c_upper = [
+        copy(upper_own, tab.at[pl.ds(8, 8)], S_TAB + 2, S_TAB + 2, after),
+        copy(upper_own, tab.at[pl.ds(40, 8)], S_TAB + 3, S_TAB + 3, before),
     ]
 
     @pl.when(jnp.logical_not(source))
@@ -256,7 +260,7 @@
 
     @pl.when(jnp.logical_not(source))
     def _():
-        for cp in c_leaves:
+        for cp in c_upper:
             cp.start()
 
     ready(w_tt)
@@ -285,7 +289,7 @@
         for m in range(1, 8):
             total = total + p1[m].astype(F32)
         p3[x] = total.astype(BF)
-        for cp in c_c + c_leaves:
+        for cp in c_c + c_upper:
             cp.start()
 
     def widen(src, dst, lo, n):
@@ -372,11 +376,6 @@
     c_gt = [
         send(gt.at[pl.ds(3, 3)], gt.at[pl.ds(0, 3)], S_GT, g_after),
         send(gt.at[pl.ds(3, 3)], gt.at[pl.ds(6, 3)], S_GT + 1, g_before),
-    ]
-
-    c_upper = [
-        send(upper_own, tab.at[pl.ds(8, 8)], S_TAB + 2, after),
-        send(upper_own, tab.at[pl.ds(40, 8)], S_TAB + 3, before),
     ]
 
     ready(w_lc)
@@ -407,12 +406,6 @@
     widen(tab, bdt, 32, 1)
     lax.fori_loop(0, 2, far_step, 0)
 
-    for cp in c_upper:
-        cp.wait_recv()
-    widen(tab, bdt, 8, 1)
-    widen(tab, bdt, 40, 1)
-    lax.fori_loop(2, 4, far_step, 0)
-
     ready(w_gc)
     for cp in c_gt:
         cp.wait_recv()
@@ -429,6 +422,12 @@
     f2 = in_order(found[2], found[2])
     f_half = jnp.where(half == 0, f01, half_swap(f01))[:, :64]
     d_half = f_half + nt(f2[:, :64].astype(BF), ge[half][:, :64])
+
+    for cp in c_upper:
+        cp.wait_recv()
+    widen(tab, bdt, 8, 1)
+    widen(tab, bdt, 40, 1)
+    lax.fori_loop(2, 4, far_step, 0)
 
     e_root = es[30 * 64 : 31 * 64, :]
     d_root = far[15][:, :64] + nt(d_half.astype(BF), e_root[:, :64])

time: 35.2 us -> 35.3 us (level)
  no operation moved by 1% of the time
where the time goes in v6:
time: 35.3 us; the launch traced here: 35.2 us
  Pallas kernels  33.5 us (95%)
  local copies, waits for them, and re-layouts  1.67 us (5%)
    pallas_call x1, Pallas kernels, body(): pl.pallas_call(kernel, out_shape=jax.ShapeDtypeStruct((64, 1024), F32), i...  33.5 us
    unnamed x1, local copies, waits for them, and re-layouts  1.67 us

profile of v6, /device:TPU:1, one launch (start us, length us, event | category | flops | bytes accessed | tf_op | source)
XLA Modules:
  0.0 35.2 jit_solution(17435244940690041269)
XLA Ops:
  0.0 33.5 %h2.1 = f32[64,1024]{1,0:T(8,128)} custom-call(s32[8,16]{1,0:T(8,128)} %bitcast.5, s32[8,31]{1,0:T(8,128)} %bitcast.6, s32[31]{0:T(128)} %local_count_hbm.1, s32[3,4]{1,0:T(4,128)} %group_partner_hbm.1, s32[3]{0:T(128)} %group_count_hbm.1, s32[3,63]{1,0:T(4,128)} %bitcast.7, s32[63]{0:T(128)} %top_count_hbm.1, bf16[64,1024]{1,0:T(8,128)(2,1)} %x_hbm.1, ...), custom_call_target="tpu_custom_call" | custom-call | tf_op jit(solution)/shard_map/h2/pallas_call | solution.py:482
  33.5 1.7 %copy.18 = f32[64,1024]{1,0:T(8,128)} copy(f32[64,1024]{1,0:T(8,128)} %h2.1) | data formatting | bytes 524288

commit v7 on v6

--- a/solution.py
+++ b/solution.py
@@ -35,7 +35,7 @@
     top_count_hbm, x_hbm, basis_hbm, near_hbm, ltrans_hbm, lcouple_hbm, gtrans_hbm, gcouple_hbm, ttrans_hbm, tcouple_hbm,
     out,
     xs, bs, nb, lt, lc, gt_in, gc, tt, tc,
-    es, ge, et, ts, bd, tab, bdt, xbd, pp,
+    es, ge, et, ts, wf, bd, tab, bdt, xbd, pp,
     qb, hr, p1, p3, p4, ub, gu, gt, gs, zb, far, nearp, vht,
     near_list, local_partner, local_count, group_partner, group_count, top_partner, top_count,
     lsem, ssem, rsem, csem,
@@ -233,7 +233,17 @@
         v = v + jnp.concatenate([seen(0, wanted[5]), seen(0, wanted[7])], axis=1)
         zb[...] = v.astype(BF)
 
+    upward()
     pl.semaphore_wait(barrier, jnp.where(source, 42, 15))
+
+    c_q = copy(qb, p1.at[member], S_Q, S_Q + member, column_peer(z))
+
+    @pl.when(jnp.logical_not(source))
+    def _():
+        c_q.start()
+
+    c_u = [send(ub, gu.at[sub], S_U + d, sub_peers[d]) for d in range(1, 4)]
+    gu[sub] = ub[...]
     c_xh = [
         send(xs.at[pl.ds(8, 4)], xs.at[pl.ds(0, 4)], S_XH, after),
         send(xs.at[pl.ds(4, 4)], xs.at[pl.ds(12, 4)], S_XH + 1, before),
@@ -243,25 +253,10 @@
         send(leaves_own, tab.at[pl.ds(0, 8)], S_TAB, after),
         send(leaves_own, tab.at[pl.ds(32, 8)], S_TAB + 1, before),
     ]
-    upward()
-
-    c_q = copy(qb, p1.at[member], S_Q, S_Q + member, column_peer(z))
     c_upper = [
-        copy(upper_own, tab.at[pl.ds(8, 8)], S_TAB + 2, S_TAB + 2, after),
-        copy(upper_own, tab.at[pl.ds(40, 8)], S_TAB + 3, S_TAB + 3, before),
+        send(upper_own, tab.at[pl.ds(8, 8)], S_TAB + 2, after),
+        send(upper_own, tab.at[pl.ds(40, 8)], S_TAB + 3, before),
     ]
-
-    @pl.when(jnp.logical_not(source))
-    def _():
-        c_q.start()
-
-    c_u = [send(ub, gu.at[sub], S_U + d, sub_peers[d]) for d in range(1, 4)]
-    gu[sub] = ub[...]
-
-    @pl.when(jnp.logical_not(source))
-    def _():
-        for cp in c_upper:
-            cp.start()
 
     ready(w_tt)
     ready(w_tc)
@@ -289,7 +284,7 @@
         for m in range(1, 8):
             total = total + p1[m].astype(F32)
         p3[x] = total.astype(BF)
-        for cp in c_c + c_upper:
+        for cp in c_c:
             cp.start()
 
     def widen(src, dst, lo, n):
@@ -380,11 +375,15 @@
 
     ready(w_lc)
 
-    def far_step(i, carry):
-        weights = []
+    def far_blocks(i, carry):
         for h in range(8):
             c = jnp.minimum(8 * i + h, 30)
-            weights.append(spread(lambda j: lc[c, :, 128 * j : 128 * j + 128], 8))
+            wf[8 * i + h] = spread(lambda j: lc[c, :, 128 * j : 128 * j + 128], 8)
+        return carry
+
+    lax.fori_loop(0, 4, far_blocks, 0)
+
+    def far_step(i, carry):
         parts = []
         for h in range(8):
             c = jnp.minimum(8 * i + h, 30)
@@ -394,7 +393,7 @@
                 e = jnp.clip(local_partner[k, c] - (b - 1) * 31, 0, 92)
                 e = e + jnp.where(e >= 31, 1, 0) + jnp.where(e >= 62, 1, 0)
                 ids.append(jnp.where(k < count, e, 63))
-            parts.append(coupled(bdt, ids, weights[h]))
+            parts.append(coupled(bdt, ids, wf[8 * i + h]))
         for h in range(4):
             far[4 * i + h] = in_order(parts[2 * h], parts[2 * h + 1])
         return carry
@@ -498,6 +497,7 @@
             vm((3, 64, 128), BF),
             vm((16 * 64, 128), BF),
             vm((18, 64, 128), BF),
+            vm((32, 64, 512), BF),
             vm((8, 128, 128), BF),
             vm((48, 64, 128), BF),
             vm((96, 128, 128), BF),

time: 35.3 us -> 33.3 us (0.943)
  Pallas kernels: 33.5 us -> 31.5 us
    pallas_call x1, Pallas kernels: 33.5 us -> 31.5 us  [body(): pl.pallas_call(kernel, out_shape=jax.ShapeDtypeStruct((64, 1024), F32), i...]
where the time goes in v7:
time: 33.3 us; the launch traced here: 33.2 us
  Pallas kernels  31.5 us (95%)
  local copies, waits for them, and re-layouts  1.67 us (5%)
    pallas_call x1, Pallas kernels, body(): pl.pallas_call(kernel, out_shape=jax.ShapeDtypeStruct((64, 1024), F32), i...  31.5 us
    unnamed x1, local copies, waits for them, and re-layouts  1.67 us

profile of v7, /device:TPU:1, one launch (start us, length us, event | category | flops | bytes accessed | tf_op | source)
XLA Modules:
  0.0 33.2 jit_solution(16990227460103028596)
XLA Ops:
  0.0 31.5 %h2.1 = f32[64,1024]{1,0:T(8,128)} custom-call(s32[8,16]{1,0:T(8,128)} %bitcast.5, s32[8,31]{1,0:T(8,128)} %bitcast.6, s32[31]{0:T(128)} %local_count_hbm.1, s32[3,4]{1,0:T(4,128)} %group_partner_hbm.1, s32[3]{0:T(128)} %group_count_hbm.1, s32[3,63]{1,0:T(4,128)} %bitcast.7, s32[63]{0:T(128)} %top_count_hbm.1, bf16[64,1024]{1,0:T(8,128)(2,1)} %x_hbm.1, ...), custom_call_target="tpu_custom_call" | custom-call | tf_op jit(solution)/shard_map/h2/pallas_call | solution.py:481
  31.5 1.7 %copy.18 = f32[64,1024]{1,0:T(8,128)} copy(f32[64,1024]{1,0:T(8,128)} %h2.1) | data formatting | bytes 524288

commit v8 on v7

--- a/solution.py
+++ b/solution.py
@@ -250,18 +250,18 @@
     ]
     leaves_own, upper_own = tab.at[pl.ds(16, 8)], tab.at[pl.ds(24, 8)]
     c_leaves = [
-        send(leaves_own, tab.at[pl.ds(0, 8)], S_TAB, after),
-        send(leaves_own, tab.at[pl.ds(32, 8)], S_TAB + 1, before),
+        copy(leaves_own, tab.at[pl.ds(0, 8)], S_TAB, S_TAB, after),
+        copy(leaves_own, tab.at[pl.ds(32, 8)], S_TAB + 1, S_TAB + 1, before),
     ]
     c_upper = [
-        send(upper_own, tab.at[pl.ds(8, 8)], S_TAB + 2, after),
-        send(upper_own, tab.at[pl.ds(40, 8)], S_TAB + 3, before),
+        copy(upper_own, tab.at[pl.ds(8, 8)], S_TAB + 2, S_TAB + 2, after),
+        copy(upper_own, tab.at[pl.ds(40, 8)], S_TAB + 3, S_TAB + 3, before),
     ]
 
-    ready(w_tt)
-    ready(w_tc)
-    ready(w_top)
-    prepare_top()
+    @pl.when(jnp.logical_not(source))
+    def _():
+        for cp in c_leaves + c_upper:
+            cp.start()
 
     c_c = [
         pltpu.make_async_remote_copy(
@@ -284,8 +284,13 @@
         for m in range(1, 8):
             total = total + p1[m].astype(F32)
         p3[x] = total.astype(BF)
-        for cp in c_c:
+        for cp in c_c + c_leaves + c_upper:
             cp.start()
+
+    ready(w_tt)
+    ready(w_tc)
+    ready(w_top)
+    prepare_top()
 
     def widen(src, dst, lo, n):
         def step(i, carry):

time: 33.3 us -> 33.4 us (level)
  no operation moved by 1% of the time
where the time goes in v8:
time: 33.4 us; the launch traced here: 33.3 us
  Pallas kernels  31.6 us (95%)
  local copies, waits for them, and re-layouts  1.67 us (5%)
    pallas_call x1, Pallas kernels, body(): pl.pallas_call(kernel, out_shape=jax.ShapeDtypeStruct((64, 1024), F32), i...  31.6 us
    unnamed x1, local copies, waits for them, and re-layouts  1.67 us

profile of v8, /device:TPU:1, one launch (start us, length us, event | category | flops | bytes accessed | tf_op | source)
XLA Modules:
  0.0 33.3 jit_solution(14462884296239455367)
XLA Ops:
  0.0 31.6 %h2.1 = f32[64,1024]{1,0:T(8,128)} custom-call(s32[8,16]{1,0:T(8,128)} %bitcast.5, s32[8,31]{1,0:T(8,128)} %bitcast.6, s32[31]{0:T(128)} %local_count_hbm.1, s32[3,4]{1,0:T(4,128)} %group_partner_hbm.1, s32[3]{0:T(128)} %group_count_hbm.1, s32[3,63]{1,0:T(4,128)} %bitcast.7, s32[63]{0:T(128)} %top_count_hbm.1, bf16[64,1024]{1,0:T(8,128)(2,1)} %x_hbm.1, ...), custom_call_target="tpu_custom_call" | custom-call | tf_op jit(solution)/shard_map/h2/pallas_call | solution.py:486
  31.6 1.7 %copy.18 = f32[64,1024]{1,0:T(8,128)} copy(f32[64,1024]{1,0:T(8,128)} %h2.1) | data formatting | bytes 524288

commit v9 on v7

--- a/solution.py
+++ b/solution.py
@@ -529,13 +529,15 @@
             pltpu.SemaphoreType.DMA((32,)),
         ],
         compiler_params=pltpu.CompilerParams(
-            collective_id=0, has_side_effects=True, vmem_limit_bytes=60 * 1024 * 1024
+            collective_id=0, has_side_effects=True, vmem_limit_bytes=48 * 1024 * 1024
         ),
         name="h2",
     )(
+        *[pltpu.with_memory_space_constraint(v, pltpu.HBM) for v in (
         near_list.T, local_partner.T, local_count, group_partner, group_count, top_partner.T, top_count,
         right_sides, leaf_basis, near_blocks, local_transfer, local_couple, group_transfer, group_couple,
         top_transfer, jnp.transpose(top_couple, (1, 0, 2)),
+        )],
     )
 
 

time: 33.3 us -> 31.6 us (0.949)
  local copies, waits for them, and re-layouts: 1.67 us -> 0.71 us
  Pallas kernels: 31.5 us -> 30.8 us
    unnamed x1, local copies, waits for them, and re-layouts: 1.67 us -> 0.71 us
    pallas_call x1, Pallas kernels: 31.5 us -> 30.8 us  [body(): pl.pallas_call(kernel, out_shape=jax.ShapeDtypeStruct((64, 1024), F32), i...]
where the time goes in v9:
time: 31.6 us; the launch traced here: 31.5 us
  Pallas kernels  30.8 us (97%)
  local copies, waits for them, and re-layouts  0.71 us (2%)
    pallas_call x1, Pallas kernels, body(): pl.pallas_call(kernel, out_shape=jax.ShapeDtypeStruct((64, 1024), F32), i...  30.8 us
    unnamed x1, local copies, waits for them, and re-layouts  0.71 us

profile of v9, /device:TPU:1, one launch (start us, length us, event | category | flops | bytes accessed | tf_op | source)
XLA Modules:
  0.0 31.5 jit_solution(2032431357737506681)
XLA Ops:
  0.0 30.8 %h2.1 = f32[64,1024]{1,0:T(8,128)S(1)} custom-call(s32[8,16]{1,0:T(8,128)} %bitcast.5, s32[8,31]{1,0:T(8,128)} %bitcast.6, s32[31]{0:T(128)} %local_count_hbm.1, s32[3,4]{1,0:T(4,128)} %group_partner_hbm.1, s32[3]{0:T(128)} %group_count_hbm.1, s32[3,63]{1,0:T(4,128)} %bitcast.7, s32[63]{0:T(128)} %top_count_hbm.1, bf16[64,1024]{1,0:T(8,128)(2,1)} %x_hbm.1, ...), custom_call_target="tpu_custom_call" | custom-call | tf_op jit(solution)/shard_map/h2/pallas_call | solution.py:481
  30.8 0.7 %copy.18 = f32[64,1024]{1,0:T(8,128)} copy(f32[64,1024]{1,0:T(8,128)S(1)} %h2.1) | data formatting | bytes 524288

commit v10 on v9

--- a/solution.py
+++ b/solution.py
@@ -244,19 +244,25 @@
 
     c_u = [send(ub, gu.at[sub], S_U + d, sub_peers[d]) for d in range(1, 4)]
     gu[sub] = ub[...]
-    c_xh = [
-        send(xs.at[pl.ds(8, 4)], xs.at[pl.ds(0, 4)], S_XH, after),
-        send(xs.at[pl.ds(4, 4)], xs.at[pl.ds(12, 4)], S_XH + 1, before),
-    ]
-    leaves_own, upper_own = tab.at[pl.ds(16, 8)], tab.at[pl.ds(24, 8)]
-    c_leaves = [
-        send(leaves_own, tab.at[pl.ds(0, 8)], S_TAB, after),
-        send(leaves_own, tab.at[pl.ds(32, 8)], S_TAB + 1, before),
-    ]
-    c_upper = [
-        send(upper_own, tab.at[pl.ds(8, 8)], S_TAB + 2, after),
-        send(upper_own, tab.at[pl.ds(40, 8)], S_TAB + 3, before),
-    ]
+
+    def exchange(ref, to_after, to_before, n, from_before, from_after, place):
+        copies = []
+        for turn in range(2):
+            back = lax.rem(sub, 2) == 1 - turn
+            cp = copy(
+                ref.at[pl.ds(jnp.where(back, to_before, to_after), n)],
+                ref.at[pl.ds(jnp.where(back, from_after, from_before), n)],
+                place + turn,
+                place + jnp.where(back, 1, 0),
+                tuple(jnp.where(back, a, c) for a, c in zip(before, after)),
+            )
+            cp.start()
+            copies.append(cp)
+        return copies
+
+    c_xh = exchange(xs, 8, 4, 4, 0, 12, S_XH)
+    c_leaves = exchange(tab, 16, 16, 8, 0, 32, S_TAB)
+    c_upper = exchange(tab, 24, 24, 8, 8, 40, S_TAB + 2)
 
     ready(w_tt)
     ready(w_tc)

time: 31.6 us -> 31.6 us (level)
  no operation moved by 1% of the time
where the time goes in v10:
time: 31.6 us; the launch traced here: 31.5 us
  Pallas kernels  30.8 us (97%)
  local copies, waits for them, and re-layouts  0.71 us (2%)
    pallas_call x1, Pallas kernels, body(): pl.pallas_call(kernel, out_shape=jax.ShapeDtypeStruct((64, 1024), F32), i...  30.8 us
    unnamed x1, local copies, waits for them, and re-layouts  0.71 us

profile of v10, /device:TPU:1, one launch (start us, length us, event | category | flops | bytes accessed | tf_op | source)
XLA Modules:
  0.0 31.5 jit_solution(2263279229229911336)
XLA Ops:
  0.0 30.8 %h2.1 = f32[64,1024]{1,0:T(8,128)S(1)} custom-call(s32[8,16]{1,0:T(8,128)} %bitcast.5, s32[8,31]{1,0:T(8,128)} %bitcast.6, s32[31]{0:T(128)} %local_count_hbm.1, s32[3,4]{1,0:T(4,128)} %group_partner_hbm.1, s32[3]{0:T(128)} %group_count_hbm.1, s32[3,63]{1,0:T(4,128)} %bitcast.7, s32[63]{0:T(128)} %top_count_hbm.1, bf16[64,1024]{1,0:T(8,128)(2,1)} %x_hbm.1, ...), custom_call_target="tpu_custom_call" | custom-call | tf_op jit(solution)/shard_map/h2/pallas_call | solution.py:487
  30.8 0.7 %copy.18 = f32[64,1024]{1,0:T(8,128)} copy(f32[64,1024]{1,0:T(8,128)S(1)} %h2.1) | data formatting | bytes 524288

commit v11 on v9

--- a/solution.py
+++ b/solution.py
@@ -316,32 +316,6 @@
     def in_order(one, two):
         return nn(jnp.concatenate([one, two], axis=1).astype(BF), pp[...])
 
-    ready(w_nb)
-    widen(xs, xbd, 4, 1)
-    for cp in c_xh:
-        cp.wait_recv()
-    for at in (0, 12):
-        for h in range(4):
-            v = xs[at + h]
-            r = half_swap(v)
-            xbd[2 * (at + h)] = jnp.concatenate([v * m_left, r * m_right], axis=0)
-            xbd[2 * (at + h) + 1] = jnp.concatenate([r * m_left, v * m_right], axis=0)
-
-    def near_step(i, carry):
-        weights = []
-        for h in range(8):
-            t = 8 * i + h
-            weights.append(spread(lambda j: nb[t, :, 128 * j : 128 * j + 128], 8))
-        parts = []
-        for h in range(8):
-            ids = [jnp.clip(near_list[k, 8 * i + h] - (b * 16 - 8), 0, 31) for k in range(8)]
-            parts.append(coupled(xbd, ids, weights[h]))
-        for h in range(4):
-            nearp[4 * i + h] = in_order(parts[2 * h], parts[2 * h + 1])
-        return carry
-
-    lax.fori_loop(0, 2, near_step, 0)
-
     c_d = [copy(p4.at[member], p4.at[member], S_D + d, S_D + d, col_peers[d]) for d in range(1, 8)]
     for i in range(4):
 
@@ -372,6 +346,32 @@
         send(gt.at[pl.ds(3, 3)], gt.at[pl.ds(0, 3)], S_GT, g_after),
         send(gt.at[pl.ds(3, 3)], gt.at[pl.ds(6, 3)], S_GT + 1, g_before),
     ]
+
+    ready(w_nb)
+    widen(xs, xbd, 4, 1)
+    for cp in c_xh:
+        cp.wait_recv()
+    for at in (0, 12):
+        for h in range(4):
+            v = xs[at + h]
+            r = half_swap(v)
+            xbd[2 * (at + h)] = jnp.concatenate([v * m_left, r * m_right], axis=0)
+            xbd[2 * (at + h) + 1] = jnp.concatenate([r * m_left, v * m_right], axis=0)
+
+    def near_step(i, carry):
+        weights = []
+        for h in range(8):
+            t = 8 * i + h
+            weights.append(spread(lambda j: nb[t, :, 128 * j : 128 * j + 128], 8))
+        parts = []
+        for h in range(8):
+            ids = [jnp.clip(near_list[k, 8 * i + h] - (b * 16 - 8), 0, 31) for k in range(8)]
+            parts.append(coupled(xbd, ids, weights[h]))
+        for h in range(4):
+            nearp[4 * i + h] = in_order(parts[2 * h], parts[2 * h + 1])
+        return carry
+
+    lax.fori_loop(0, 2, near_step, 0)
 
     ready(w_lc)
 

time: 31.6 us -> 33.2 us (1.051)
  Pallas kernels: 30.8 us -> 32.4 us
    pallas_call x1, Pallas kernels: 30.8 us -> 32.4 us  [body(): pl.pallas_call(kernel, out_shape=jax.ShapeDtypeStruct((64, 1024), F32), i...]
where the time goes in v11:
time: 33.2 us; the launch traced here: 33.1 us
  Pallas kernels  32.4 us (98%)
  local copies, waits for them, and re-layouts  0.71 us (2%)
    pallas_call x1, Pallas kernels, body(): pl.pallas_call(kernel, out_shape=jax.ShapeDtypeStruct((64, 1024), F32), i...  32.4 us
    unnamed x1, local copies, waits for them, and re-layouts  0.71 us

profile of v11, /device:TPU:1, one launch (start us, length us, event | category | flops | bytes accessed | tf_op | source)
XLA Modules:
  0.0 33.1 jit_solution(7449849779285232000)
XLA Ops:
  0.0 32.4 %h2.1 = f32[64,1024]{1,0:T(8,128)S(1)} custom-call(s32[8,16]{1,0:T(8,128)} %bitcast.5, s32[8,31]{1,0:T(8,128)} %bitcast.6, s32[31]{0:T(128)} %local_count_hbm.1, s32[3,4]{1,0:T(4,128)} %group_partner_hbm.1, s32[3]{0:T(128)} %group_count_hbm.1, s32[3,63]{1,0:T(4,128)} %bitcast.7, s32[63]{0:T(128)} %top_count_hbm.1, bf16[64,1024]{1,0:T(8,128)(2,1)} %x_hbm.1, ...), custom_call_target="tpu_custom_call" | custom-call | tf_op jit(solution)/shard_map/h2/pallas_call | solution.py:481
  32.4 0.7 %copy.18 = f32[64,1024]{1,0:T(8,128)} copy(f32[64,1024]{1,0:T(8,128)S(1)} %h2.1) | data formatting | bytes 524288
